TPU v7x, 32 devices: a whole 2x2x4 slice. The times are simulated.
32 devices in a mesh: dp: 8 (over y, x, core), tensor: 4 (over z).
Axes of the slice: x: 2, y: 2, z: 4, core: 2. Of those that a mesh axis runs over, the one named last changes fastest.
Arguments:
- tokens: bfloat16 [16384, 767], P(('dp', 'tensor')), may hold values from -6 to 6
- cotangent: bfloat16 [16384, 767], P(('dp', 'tensor')), may hold values from -6 to 6
- seq_length: int32 [8], P('dp'), may hold values from 512 to 2048, as said below
- live_rows: int32 [8], P('dp'), may hold values from 512 to 2048, as said below
- qkv_weight: bfloat16 [767, 3, 768], P(None, None, 'tensor'), may hold values from -0.21875 to 0.21875
- qv_bias: bfloat16 [2, 768], P(None, 'tensor'), may hold values from -1.75 to 1.75
- out_weight: bfloat16 [768, 767], P('tensor'), may hold values from -0.875 to 0.875
- out_bias: bfloat16 [767], replicated, may hold values from -1.75 to 1.75
- up_weight: bfloat16 [767, 3072], P(None, 'tensor'), may hold values from -0.21875 to 0.21875
- up_bias: bfloat16 [3072], P('tensor'), may hold values from -1.75 to 1.75
- down_weight: bfloat16 [3072, 767], P('tensor'), may hold values from -0.109375 to 0.109375
- down_bias: bfloat16 [767], replicated, may hold values from -1.75 to 1.75
Outputs:
- mixed: bfloat16 [16384, 767], P(('dp', 'tensor'))
- token_grad: bfloat16 [16384, 767], P(('dp', 'tensor'))
- qkv_weight_grad: float32 [767, 3, 768], P(None, None, 'tensor')
- qv_bias_grad: float32 [2, 768], P(None, 'tensor')
- out_weight_grad: float32 [768, 767], P('tensor')
- out_bias_grad: float32 [767], replicated
- up_weight_grad: float32 [767, 3072], P(None, 'tensor')
- up_bias_grad: float32 [3072], P('tensor')
- down_weight_grad: float32 [3072, 767], P('tensor')
- down_bias_grad: float32 [767], replicated
Inputs may be any that keep to these rules, and one draw needn't show every extreme that they name: Index j of dp holds 2048 / seq_length[j] sequences of seq_length[j] rows each, back to back; seq_length is 2048, 1024 or 512, and each of the three occurs on some index. Rows of index j at or past live_rows[j] are padding; some index has seq_length = live_rows = 2048.
All inputs are finite; a program needn't handle non-finite values.
Results may differ from a plain program's by a relative error of at most 0.0071.
Values may be sent and summed in bfloat16 or wider, within the bound.
A program may use at most 192 MiB of HBM per device.

v0:
```python
from functools import partial

import jax
import jax.numpy as jnp
from jax import lax
from jax.sharding import PartitionSpec as P

HEAD = 64


EPSILON = 1e-05
NEGATIVE = -1e30
HIGHEST_PRECISION = lax.Precision.HIGHEST
ROW_CONTRACT = (((0,), (0,)), ((), ()))
COL_CONTRACT = (((1,), (1,)), ((), ()))


def compressed_norm(values):
    total = jnp.sum(values, axis=-1, keepdims=True)
    power = (jnp.sum(values * values, axis=-1, keepdims=True) + total * total) / (
        values.shape[-1] + 1
    )
    return values * lax.rsqrt(power + EPSILON)


def norm_back(values, upstream):
    outcome, pullback = jax.vjp(compressed_norm, values)
    return pullback(upstream)[0]


def gelu_tanh(values):
    return jax.nn.gelu(values, approximate=True)


def gelu_back(values, upstream):
    outcome, pullback = jax.vjp(gelu_tanh, values)
    return pullback(upstream)[0]


def keep_state(state):
    return state


def block_needed(row_block, key_block, block_rows, seq_len, live_count):
    first_key = key_block * block_rows
    return (row_block * block_rows // seq_len == first_key // seq_len) & (first_key < live_count)


def block_scores(queries, keyed, row_block, key_block, block_rows, seq_len, live_count):
    query_rows = queries[row_block * block_rows : (row_block + 1) * block_rows]
    key_rows = keyed[key_block * block_rows : (key_block + 1) * block_rows]
    scaling = queries.shape[-1] ** (-0.5)
    raw_scores = (
        jnp.einsum("qhd,khd->hqk", query_rows, key_rows, preferred_element_type=jnp.float32)
        * scaling
    )
    query_pos = row_block * block_rows + jnp.arange(block_rows, dtype=jnp.int32)
    key_pos = key_block * block_rows + jnp.arange(block_rows, dtype=jnp.int32)
    same_seq = query_pos[:, None] // seq_len == key_pos[None, :] // seq_len
    causal = key_pos[None, :] <= query_pos[:, None]
    alive = (key_pos[None, :] < live_count) | (key_pos[None, :] == query_pos[:, None])
    return jnp.where((same_seq & causal & alive)[None], raw_scores, NEGATIVE)


def over_keys(row_block, block_rows, seq_len, live_count, update, state):
    for key_block in range(row_block + 1):
        advance = partial(update, key_block)
        if key_block == row_block:
            state = advance(state)
        else:
            state = lax.cond(
                block_needed(row_block, key_block, block_rows, seq_len, live_count),
                advance,
                keep_state,
                state,
            )
    return state


def split_qkv(qkv):
    row_count = qkv.shape[0]
    parts = qkv.reshape(row_count, 3, -1, HEAD)
    return (parts[:, 0], parts[:, 1], parts[:, 2])


def attention(qkv, seq_len, live_count):
    row_count = qkv.shape[0]
    queries, keyed, valued = split_qkv(qkv)
    heads = queries.shape[1]
    block_rows = row_count // 4
    lse_blocks, out_blocks, exact_blocks = ([], [], [])
    for row_block in range(4):

        def stat_update(key_block, state, row_block=row_block):
            top_old, mass_old = state
            scores = block_scores(
                queries, keyed, row_block, key_block, block_rows, seq_len, live_count
            )
            top_new = jnp.maximum(top_old, jnp.max(scores, axis=-1))
            mass_new = mass_old * jnp.exp(top_old - top_new) + jnp.sum(
                jnp.exp(scores - top_new[..., None]), axis=-1
            )
            return (top_new, mass_new)

        initial = (
            jnp.full((heads, block_rows), NEGATIVE, jnp.float32),
            jnp.zeros((heads, block_rows), jnp.float32),
        )
        top_final, mass_final = over_keys(
            row_block, block_rows, seq_len, live_count, stat_update, initial
        )
        log_mass = top_final + jnp.log(mass_final)

        def out_update(key_block, state, row_block=row_block, log_mass=log_mass):
            mixed_old, exact_old = state
            scores = block_scores(
                queries, keyed, row_block, key_block, block_rows, seq_len, live_count
            )
            softmaxed = jnp.exp(scores - log_mass[..., None])
            value_rows = valued[key_block * block_rows : (key_block + 1) * block_rows]
            mixed_new = mixed_old + jnp.einsum(
                "hqk,khd->qhd",
                softmaxed.astype(jnp.bfloat16),
                value_rows,
                preferred_element_type=jnp.float32,
            )
            exact_new = exact_old + jnp.einsum(
                "hqk,khd->qhd",
                softmaxed,
                value_rows.astype(jnp.float32),
                precision=HIGHEST_PRECISION,
                preferred_element_type=jnp.float32,
            )
            return (mixed_new, exact_new)

        zeros_block = jnp.zeros((block_rows, heads, HEAD), jnp.float32)
        mixed_final, exact_final = over_keys(
            row_block, block_rows, seq_len, live_count, out_update, (zeros_block, zeros_block)
        )
        lse_blocks.append(log_mass)
        out_blocks.append(mixed_final.astype(jnp.bfloat16))
        exact_blocks.append(exact_final)
    heads_out = jnp.concatenate(out_blocks, axis=0).reshape(row_count, heads * HEAD)
    return (jnp.concatenate(lse_blocks, axis=1), heads_out, jnp.concatenate(exact_blocks, axis=0))


def attention_back(qkv, log_mass, exact, head_grads, seq_len, live_count):
    row_count = qkv.shape[0]
    queries, keyed, valued = split_qkv(qkv)
    heads = queries.shape[1]
    block_rows = row_count // 4
    grad_heads = head_grads.reshape(row_count, heads, HEAD)
    delta = jnp.sum(grad_heads.astype(jnp.float32) * exact, axis=-1).T
    scaling = HEAD ** (-0.5)
    zeros_block = jnp.zeros((block_rows, heads, HEAD), jnp.float32)
    key_grads = [zeros_block] * 4
    value_grads = [zeros_block] * 4
    query_grads = []
    for row_block in range(4):

        def back_update(key_block, state, row_block=row_block):
            query_acc, key_acc, value_acc = state
            lower = row_block * block_rows
            upper_row = lower + block_rows
            key_low = key_block * block_rows
            scores = block_scores(
                queries, keyed, row_block, key_block, block_rows, seq_len, live_count
            )
            softmaxed = jnp.exp(scores - log_mass[:, lower:upper_row][..., None])
            grad_rows = grad_heads[lower:upper_row]
            query_rows = queries[lower:upper_row]
            key_rows = keyed[key_low : key_low + block_rows]
            value_rows = valued[key_low : key_low + block_rows]
            prob_grads = jnp.einsum(
                "qhd,khd->hqk", grad_rows, value_rows, preferred_element_type=jnp.float32
            )
            score_grads = (softmaxed * (prob_grads - delta[:, lower:upper_row][..., None])).astype(
                jnp.bfloat16
            )
            query_new = (
                query_acc
                + jnp.einsum(
                    "hqk,khd->qhd", score_grads, key_rows, preferred_element_type=jnp.float32
                )
                * scaling
            )
            key_new = (
                key_acc
                + jnp.einsum(
                    "hqk,qhd->khd", score_grads, query_rows, preferred_element_type=jnp.float32
                )
                * scaling
            )
            value_new = value_acc + jnp.einsum(
                "hqk,qhd->khd",
                softmaxed.astype(jnp.bfloat16),
                grad_rows,
                preferred_element_type=jnp.float32,
            )
            return (query_new, key_new, value_new)

        query_acc = zeros_block
        for key_block in range(row_block + 1):
            advance = partial(back_update, key_block)
            state = (query_acc, key_grads[key_block], value_grads[key_block])
            if key_block == row_block:
                state = advance(state)
            else:
                state = lax.cond(
                    block_needed(row_block, key_block, block_rows, seq_len, live_count),
                    advance,
                    keep_state,
                    state,
                )
            query_acc, key_grads[key_block], value_grads[key_block] = state
        query_grads.append(query_acc)
    stacked = jnp.stack(
        [
            jnp.concatenate(query_grads, axis=0),
            jnp.concatenate(key_grads, axis=0),
            jnp.concatenate(value_grads, axis=0),
        ],
        axis=1,
    )
    return stacked.reshape(row_count, -1).astype(jnp.bfloat16)


def local(
    tokens,
    cotangent,
    seq_length,
    live_rows,
    qkv_weight,
    qv_bias,
    out_weight,
    out_bias,
    up_weight,
    up_bias,
    down_weight,
    down_bias,
):
    seq_len = seq_length[0]
    live_count = live_rows[0]
    inputs = tokens.astype(jnp.float32)
    norm_one = compressed_norm(inputs).astype(jnp.bfloat16)
    qkv_flat = qkv_weight.reshape(qkv_weight.shape[0], -1)
    qkv_shift = jnp.concatenate([qv_bias[0], jnp.zeros_like(qv_bias[0]), qv_bias[1]]).astype(
        jnp.float32
    )
    qkv = (
        jnp.dot(
            lax.all_gather(norm_one, "tensor", axis=0, tiled=True),
            qkv_flat,
            preferred_element_type=jnp.float32,
        )
        + qkv_shift
    ).astype(jnp.bfloat16)
    log_mass, heads_out, exact = attention(qkv, seq_len, live_count)
    attn_part = lax.psum_scatter(
        jnp.dot(heads_out, out_weight, preferred_element_type=jnp.float32),
        "tensor",
        scatter_dimension=0,
        tiled=True,
    )
    hidden = inputs + attn_part + out_bias.astype(jnp.float32)
    norm_two = compressed_norm(hidden).astype(jnp.bfloat16)
    up_shift = up_bias.astype(jnp.float32)
    pre_act = (
        jnp.dot(
            lax.all_gather(norm_two, "tensor", axis=0, tiled=True),
            up_weight,
            preferred_element_type=jnp.float32,
        )
        + up_shift
    )
    activated = gelu_tanh(pre_act).astype(jnp.bfloat16)
    mixed = (
        hidden
        + lax.psum_scatter(
            jnp.dot(activated, down_weight, preferred_element_type=jnp.float32),
            "tensor",
            scatter_dimension=0,
            tiled=True,
        )
        + down_bias.astype(jnp.float32)
    ).astype(jnp.bfloat16)
    grad_out = cotangent.astype(jnp.float32)
    full_grad = lax.all_gather(cotangent, "tensor", axis=0, tiled=True)
    down_weight_grad = lax.dot_general(
        activated, full_grad, ROW_CONTRACT, preferred_element_type=jnp.float32
    )
    act_grad = lax.dot_general(
        full_grad, down_weight, COL_CONTRACT, preferred_element_type=jnp.float32
    )
    pre_grad = gelu_back(pre_act, act_grad).astype(jnp.bfloat16)
    up_bias_grad = jnp.sum(pre_grad.astype(jnp.float32), axis=0)
    matched = pre_grad
    up_weight_grad = lax.dot_general(
        lax.all_gather(norm_two, "tensor", axis=0, tiled=True),
        matched,
        ROW_CONTRACT,
        preferred_element_type=jnp.float32,
    )
    norm_two_grad = lax.psum_scatter(
        lax.dot_general(pre_grad, up_weight, COL_CONTRACT, preferred_element_type=jnp.float32),
        "tensor",
        scatter_dimension=0,
        tiled=True,
    )
    hidden_grad = grad_out + norm_back(hidden, norm_two_grad)
    attn_grad = hidden_grad.astype(jnp.bfloat16)
    full_attn = lax.all_gather(attn_grad, "tensor", axis=0, tiled=True)
    out_weight_grad = lax.dot_general(
        heads_out, full_attn, ROW_CONTRACT, preferred_element_type=jnp.float32
    )
    head_grads = lax.dot_general(
        full_attn, out_weight, COL_CONTRACT, preferred_element_type=jnp.float32
    ).astype(jnp.bfloat16)
    qkv_grad = attention_back(qkv, log_mass, exact, head_grads, seq_len, live_count)
    part_sums = jnp.sum(qkv_grad.astype(jnp.float32).reshape(qkv_grad.shape[0], 3, -1), axis=0)
    qv_bias_grad = jnp.stack([part_sums[0], part_sums[2]])
    matched = qkv_grad
    qkv_weight_grad = lax.dot_general(
        lax.all_gather(norm_one, "tensor", axis=0, tiled=True),
        matched,
        ROW_CONTRACT,
        preferred_element_type=jnp.float32,
    ).reshape(qkv_weight.shape)
    norm_one_grad = lax.psum_scatter(
        lax.dot_general(qkv_grad, qkv_flat, COL_CONTRACT, preferred_element_type=jnp.float32),
        "tensor",
        scatter_dimension=0,
        tiled=True,
    )
    token_grad = (hidden_grad + norm_back(inputs, norm_one_grad)).astype(jnp.bfloat16)
    out_bias_grad, down_bias_grad = lax.psum(
        (jnp.sum(hidden_grad, axis=0), jnp.sum(grad_out, axis=0)), ("dp", "tensor")
    )
    (
        qkv_weight_grad,
        qv_bias_grad,
        out_weight_grad,
        up_weight_grad,
        up_bias_grad,
        down_weight_grad,
    ) = lax.psum(
        (
            qkv_weight_grad,
            qv_bias_grad,
            out_weight_grad,
            up_weight_grad,
            up_bias_grad,
            down_weight_grad,
        ),
        "dp",
    )
    return (
        mixed,
        token_grad,
        qkv_weight_grad,
        qv_bias_grad,
        out_weight_grad,
        out_bias_grad,
        up_weight_grad,
        up_bias_grad,
        down_weight_grad,
        down_bias_grad,
    )


def solution(mesh):
    placed = (
        P(("dp", "tensor"), None),
        P(("dp", "tensor"), None),
        P("dp"),
        P("dp"),
        P(None, None, "tensor"),
        P(None, "tensor"),
        P("tensor", None),
        P(),
        P(None, "tensor"),
        P("tensor"),
        P("tensor", None),
        P(),
    )
    return jax.shard_map(
        local,
        mesh=mesh,
        in_specs=placed,
        out_specs=(
            P(("dp", "tensor"), None),
            P(("dp", "tensor"), None),
            P(None, None, "tensor"),
            P(None, "tensor"),
            P("tensor", None),
            P(),
            P(None, "tensor"),
            P("tensor"),
            P("tensor", None),
            P(),
        ),
        check_vma=False,
    )
```

profile of v0, /device:TPU:0, one launch (start us, length us, event | category | flops | bytes accessed | tf_op | source)
XLA Modules:
  0.0 1115.4 jit_solution(13469163770344121325)
XLA Ops:
  15.2 62.2 %all-gather.5.cloned.1.call-done = bf16[2048,767]{1,0:T(8,128)(2,1)} async-done(((bf16[512,767]{1,0:T(8,128)(2,1)}), bf16[2048,767]{1,0:T(8,128)(2,1)}) %all-gather.5.cloned.1.call-update) | async-done | bytes 3141648 | tf_op jit(solution)/shard_map/all_gather | solution.py:252
  77.4 4.1 add_convert_fusion
  91.7 7.5 conditional.29
  99.2 3.6 fusion.448
  112.8 3.6 fusion.449
  119.9 5.3 conditional.18
  129.2 7.7 conditional.19
  150.3 171.6 %reduce-scatter.5.cloned.1.call-done = f32[512,767]{1,0:T(8,128)} async-done(((f32[2048,767]{1,0:T(8,128)}), f32[512,767]{1,0:T(8,128)}) %reduce-scatter.5.cloned.1.call-update) | async-done | bytes 1570832 | tf_op jit(solution)/shard_map/reduce_scatter | solution.py:259
  326.6 62.6 %all-gather.7.cloned.1.call-done = bf16[2048,767]{1,0:T(8,128)(2,1)} async-done(((bf16[512,767]{1,0:T(8,128)(2,1)}), bf16[2048,767]{1,0:T(8,128)(2,1)}) %all-gather.7.cloned.1.call-update) | async-done | bytes 3141648 | tf_op jit(solution)/shard_map/all_gather | solution.py:270
  389.2 7.4 fusion.492
  396.6 56.2 %all-gather.9.cloned.1.call-done = bf16[2048,767]{1,0:T(8,128)(2,1)} async-done(((bf16[512,767]{1,0:T(8,128)(2,1)}), bf16[2048,767]{1,0:T(8,128)(2,1)}) %all-gather.9.cloned.1.call-update) | async-done | bytes 3141648 | tf_op jit(solution)/shard_map/all_gather | solution.py:288
  452.8 11.1 convert_reduce_fusion
  465.6 4.5 fusion.494
  470.2 7.3 fusion.493
  478.1 101.5 %reduce-scatter.9.cloned.1.call-done = f32[512,767]{1,0:T(8,128)} async-done(((f32[2048,767]{1,0:T(8,128)}), f32[512,767]{1,0:T(8,128)}) %reduce-scatter.9.cloned.1.call-update) | async-done | bytes 1570832 | tf_op jit(solution)/shard_map/reduce_scatter | solution.py:304
  581.3 111.8 %reduce-scatter.7.cloned.1.call-done = f32[512,767]{1,0:T(8,128)} async-done(((f32[2048,767]{1,0:T(8,128)}), f32[512,767]{1,0:T(8,128)}) %reduce-scatter.7.cloned.1.call-update) | async-done | bytes 1570832 | tf_op jit(solution)/shard_map/reduce_scatter | solution.py:279
  699.2 4.1 fusion.430
  703.4 4.0 fusion.436
  707.4 4.0 fusion.435
  711.5 3.7 fusion.434
  715.2 47.8 %all-gather.11.cloned.1.call-done = bf16[2048,767]{1,0:T(8,128)(2,1)} async-done(((bf16[512,767]{1,0:T(8,128)(2,1)}), bf16[2048,767]{1,0:T(8,128)(2,1)}) %all-gather.11.cloned.1.call-update) | async-done | bytes 3141648 | tf_op jit(solution)/shard_map/all_gather | solution.py:312
  776.6 10.0 conditional.30
  786.6 3.9 convolution_bitcast_fusion.2
  795.5 3.9 convolution_bitcast_fusion.1
  804.3 3.7 convolution_bitcast_fusion
  822.6 4.5 fusion.495
  827.2 7.2 fusion.498
  834.4 4.1 fusion.497
  843.5 90.2 %all-reduce = (f32[767]{0:T(1024)}, f32[767]{0:T(1024)}) all-reduce(f32[767]{0:T(1024)S(1)} %get-tuple-element.573, f32[767]{0:T(1024)S(1)} %get-tuple-element.655), channel_id=1, replica_groups=mesh['dp'=8,'tensor'=4] {'dp','tensor'}, use_global_device_ids=true, to_apply=%region_72.73 | all-reduce | flops 1534 | bytes 12272 | tf_op jit(solution)/shard_map/psum | solution.py:336
  933.9 14.3 %all-reduce.1 = (f32[2,192]{1,0:T(2,128)}, f32[768]{0:T(1024)}) all-reduce(f32[2,192]{1,0:T(2,128)S(1)} %pad_maximum_fusion.1, f32[768]{0:T(1024)S(1)} %copy-done.90), channel_id=1, replica_groups=mesh['dp'=8,'tensor'=4] {'dp'}, use_global_device_ids=true, to_apply=%region_69.70 | all-reduce | flops 1152 | bytes 9216 | tf_op jit(solution)/shard_map/psum | solution.py:346
  948.2 35.6 %reduce-scatter.11.cloned.1.call-done = f32[512,767]{1,0:T(8,128)} async-done(((f32[2048,767]{1,0:T(8,128)}), f32[512,767]{1,0:T(8,128)}) %reduce-scatter.11.cloned.1.call-update) | async-done | bytes 1570832 | tf_op jit(solution)/shard_map/reduce_scatter | solution.py:329
  987.0 115.1 %all-reduce.5.cloned.1.call-done = (f32[767,3,192]{0,2,1:T(8,128)}, f32[192,767]{1,0:T(8,128)}, f32[767,768]{1,0:T(8,128)}, f32[768,767]{1,0:T(8,128)}) async-done(((f32[767,3,192]{0,2,1:T(8,128)}, f32[192,767]{1,0:T(8,128)}, f32[767,768]{1,0:T(8,128)}, f32[768,767]{1,0:T(8,128)}), (f32[767,3,192]{0,2,1:T(8,128)}, f32[192,767]{1,0:T(8,128)}, f32[767,768]{1,0:T(8,128)}, ...) | async-done | bytes 7068688 | tf_op jit(solution)/shard_map/psum | solution.py:346
  (325 shorter events, 139.4 us)
Async XLA Ops:
  7.2 445.6 %copy-start = (bf16[768,767]{1,0:T(8,128)(2,1)S(1)}, bf16[768,767]{1,0:T(8,128)(2,1)}, u32[]{:S(2)}) copy-start(bf16[768,767]{1,0:T(8,128)(2,1)} %param.58) | copy-start | bytes 3534340
  7.2 70.2 %all-gather.5.cloned.1.call-start = ((), (), s32[]{:S(2)}) async-start(), calls=%async_computation.4 | async-start | bytes 3932160 | tf_op jit(solution)/shard_map/all_gather | solution.py:252
  8.8 72.8 %copy-start.72 = (f32[512]{0:T(512)}, f32[512]{0:T(512)S(1)}, u32[]{:S(2)}) copy-start(f32[512]{0:T(512)S(1)} %fusion.466) | copy-start | bytes 6148
  11.1 310.9 %reduce-scatter.5.cloned.1.call-start = ((), (), s32[]{:S(2)}) async-start(), calls=%async_computation.5 | async-start | bytes 7864320 | tf_op jit(solution)/shard_map/reduce_scatter | solution.py:259
  14.4 122.5 %copy-start.44 = (pred[512,512]{0,1:T(8,128)(4,1)}, pred[512,512]{0,1:T(8,128)(4,1)S(1)}, u32[]{:S(2)}) copy-start(pred[512,512]{0,1:T(8,128)(4,1)S(1)} %or_and_fusion.11) | copy-start | bytes 786436
  14.8 84.4 %copy-start.38 = (pred[512,512]{0,1:T(8,128)(4,1)}, pred[512,512]{0,1:T(8,128)(4,1)S(1)}, u32[]{:S(2)}) copy-start(pred[512,512]{0,1:T(8,128)(4,1)S(1)} %or_and_fusion.9) | copy-start | bytes 786436
  15.2 97.6 %copy-start.41 = (pred[512,512]{0,1:T(8,128)(4,1)}, pred[512,512]{0,1:T(8,128)(4,1)S(1)}, u32[]{:S(2)}) copy-start(pred[512,512]{0,1:T(8,128)(4,1)S(1)} %or_and_fusion.10) | copy-start | bytes 786436
  82.9 46.3 %copy-start.2 = (bf16[2048,3,64]{0,2,1:T(8,128)(2,1)}, bf16[2048,3,64]{0,2,1:T(8,128)(2,1)S(1)}, u32[]{:S(2)}) copy-start(bf16[2048,3,64]{0,2,1:T(8,128)(2,1)S(1)} %get-tuple-element.653) | copy-start | bytes 2359300
  89.9 9.3 copy-start.78
  129.2 7.7 copy-start.84
  149.6 239.5 %all-gather.7.cloned.1.call-start = ((), (), s32[]{:S(2)}) async-start(), calls=%async_computation.6 | async-start | bytes 3932160 | tf_op jit(solution)/shard_map/all_gather | solution.py:270
  325.0 127.8 %all-gather.9.cloned.1.call-start = ((), (), s32[]{:S(2)}) async-start(), calls=%async_computation.8 | async-start | bytes 3932160 | tf_op jit(solution)/shard_map/all_gather | solution.py:288
  325.6 254.0 %reduce-scatter.9.cloned.1.call-start = ((), (), s32[]{:S(2)}) async-start(), calls=%async_computation.9 | async-start | bytes 7864320 | tf_op jit(solution)/shard_map/reduce_scatter | solution.py:304
  452.8 12.8 %copy-start.96 = (bf16[767,768]{1,0:T(8,128)(2,1)S(1)}, bf16[767,768]{1,0:T(8,128)(2,1)}, u32[]{:S(2)}) copy-start(bf16[767,768]{1,0:T(8,128)(2,1)} %param.56) | copy-start | bytes 3534340
  470.1 223.0 %reduce-scatter.7.cloned.1.call-start = ((), (), s32[]{:S(2)}) async-start(), calls=%async_computation.7 | async-start | bytes 7864320 | tf_op jit(solution)/shard_map/reduce_scatter | solution.py:279
  477.5 215.6 %copy-start.16 = (bf16[512,767]{1,0:T(8,128)(2,1)S(1)}, bf16[512,767]{1,0:T(8,128)(2,1)}, u32[]{:S(2)}) copy-start(bf16[512,767]{1,0:T(8,128)(2,1)} %param.49) | copy-start | bytes 2356228
  477.5 285.4 %all-gather.11.cloned.1.call-start = ((), (), s32[]{:S(2)}) async-start(), calls=%async_computation.10 | async-start | bytes 3932160 | tf_op jit(solution)/shard_map/all_gather | solution.py:312
  698.7 285.1 %reduce-scatter.11.cloned.1.call-start = ((), (), s32[]{:S(2)}) async-start(), calls=%async_computation.11 | async-start | bytes 7864320 | tf_op jit(solution)/shard_map/reduce_scatter | solution.py:329
  715.2 51.8 %copy-start.59 = (f32[512,3,64]{0,2,1:T(8,128)S(1)}, f32[512,3,64]{0,2,1:T(8,128)}, u32[]{:S(2)}) copy-start(f32[512,3,64]{0,2,1:T(8,128)} %fusion.436) | copy-start | bytes 1179652
  766.1 10.5 copy-start.26
  786.6 6.0 copy-start.36
  810.3 6.6 copy-start.15
  827.1 275.0 %all-reduce.5.cloned.1.call-start = ((), (), s32[]{:S(2)}) async-start(), calls=%async_computation.12 | async-start | bytes 14155776 | tf_op jit(solution)/shard_map/psum | solution.py:346
  827.2 7.2 copy-start.95
  827.2 7.2 copy-start.99
  834.4 5.8 copy-start.94
  843.4 90.5 %copy-start.90 = (f32[768]{0:T(1024)S(1)}, f32[768]{0:T(1024)}, u32[]{:S(2)}) copy-start(f32[768]{0:T(1024)} %get-tuple-element.575) | copy-start | bytes 9220
  843.4 140.4 %copy-start.4 = (bf16[512,767]{1,0:T(8,128)(2,1)S(1)}, bf16[512,767]{1,0:T(8,128)(2,1)}, u32[]{:S(2)}) copy-start(bf16[512,767]{1,0:T(8,128)(2,1)} %param.48) | copy-start | bytes 2356228
  843.4 142.1 %copy-start.75 = (f32[512]{0:T(512)S(1)}, f32[512]{0:T(512)}, u32[]{:S(2)}) copy-start(f32[512]{0:T(512)} %copy-done.74) | copy-start | bytes 6148
  843.4 142.1 %copy-start.77 = (f32[512]{0:T(512)S(1)}, f32[512]{0:T(512)}, u32[]{:S(2)}) copy-start(f32[512]{0:T(512)} %copy-done.76) | copy-start | bytes 6148
  843.4 142.2 %copy-start.6 = (f32[512,767]{1,0:T(8,128)S(1)}, f32[512,767]{1,0:T(8,128)}, u32[]{:S(2)}) copy-start(f32[512,767]{1,0:T(8,128)} %copy-done.5) | copy-start | bytes 4712452
  843.4 142.2 %copy-start.73 = (f32[512]{0:T(512)S(1)}, f32[512]{0:T(512)}, u32[]{:S(2)}) copy-start(f32[512]{0:T(512)} %copy-done.72) | copy-start | bytes 6148
  (65 other events, 208.9 us)
Sparse Core Ops, SparseCore 0:
  11.2 66.2 all-gather.4
  149.8 172.1 reduce-scatter.4
  325.1 63.9 all-gather.6
  390.6 62.1 all-gather.8
  470.2 109.3 reduce-scatter.8
  581.8 111.2 reduce-scatter.6
  698.9 64.0 all-gather.10
  827.2 156.5 reduce-scatter.10
  988.1 113.9 all-reduce.4
where the time goes:
time: 1130 us; the launch traced here: 1120 us
  waiting for transfers between devices  765 us (68%)
  matrix products  151 us (13%)
  blocking collectives  105 us (9%)
  other arithmetic  42.4 us (4%)
  local copies, waits for them, and re-layouts  23.6 us (2%)
  between operations  16.6 us (1%)
    reduce_scatter x1, waiting for transfers between devices, local(): lax.psum_scatter(jnp.dot(heads_out, out_weight, preferred_element_type=jn...  172 us
    psum x1, waiting for transfers between devices, local(): lax.psum((qkv_weight_grad, qv_bias_grad, out_weight_grad, up_weight_grad,...  115 us
    reduce_scatter x1, waiting for transfers between devices, local(): lax.psum_scatter(jnp.dot(activated, down_weight, preferred_element_type=j...  112 us
    reduce_scatter x1, waiting for transfers between devices, local(): lax.psum_scatter(lax.dot_general(pre_grad, up_weight, COL_CONTRACT, prefe...  102 us
    psum x1, blocking collectives, local(): lax.psum((jnp.sum(hidden_grad, axis=0), jnp.sum(grad_out, axis=0)), ('dp'...  90.2 us
    all_gather x1, waiting for transfers between devices, local(): lax.all_gather(norm_two, 'tensor', axis=0, tiled=True)  62.6 us
    all_gather x1, waiting for transfers between devices, local(): lax.all_gather(norm_one, 'tensor', axis=0, tiled=True)  62.2 us
    all_gather x1, waiting for transfers between devices, local(): full_grad = lax.all_gather(cotangent, 'tensor', axis=0, tiled=True)  56.2 us
  transfers between devices with their start and end apart: 9, of which 9 were waited for; matrix products, arithmetic and copies ran while one was open for 5% of the time, Pallas kernels for 0%

commit v1 on v0

v1 whole, which is shorter than its diff:
```python
from functools import partial

import jax
import jax.numpy as jnp
from jax import lax
from jax.experimental import pallas as pl
from jax.experimental.pallas import tpu as pltpu
from jax.sharding import PartitionSpec as P

HEAD = 64
LANES = 128
EPSILON = 1e-05
HIDE = -1e30
BF = jnp.bfloat16
F32 = jnp.float32
BOTH = ("dp", "tensor")
VMEM = pl.BlockSpec(memory_space=pltpu.VMEM)
SMEM = pl.BlockSpec(memory_space=pltpu.SMEM)
ANY = pl.BlockSpec(memory_space=pl.ANY)
LIMIT = 60 * 1024 * 1024


def nn(a, b):
    return lax.dot_general(a, b, (((1,), (0,)), ((), ())), preferred_element_type=F32)


def nt(a, b):
    return lax.dot_general(a, b, (((1,), (1,)), ((), ())), preferred_element_type=F32)


def tn(a, b):
    return lax.dot_general(a, b, (((0,), (0,)), ((), ())), preferred_element_type=F32)


def lane_ids(rows):
    return lax.broadcasted_iota(jnp.int32, (rows, LANES), 1)


def half_turn(x):
    return pltpu.roll(x, HEAD, 1)


def fold(x):
    half = x.shape[0] // 2
    return jnp.where(lane_ids(half) < HEAD, x[:half], half_turn(x[half:]))


def unfold(x):
    low = lane_ids(x.shape[0]) < HEAD
    zero = jnp.zeros_like(x)
    return jnp.concatenate(
        [jnp.where(low, x, zero), jnp.where(low, half_turn(x), zero)], axis=0
    )


def split3(x):
    high = x.astype(BF).astype(F32)
    rest = x - high
    mid = rest.astype(BF).astype(F32)
    return high, mid, rest - mid


def norm_stats(x, width):
    s1 = jnp.sum(x, axis=-1, keepdims=True)
    s2 = jnp.sum(x * x, axis=-1, keepdims=True)
    return s1, lax.rsqrt((s2 + s1 * s1) / width + EPSILON)


def norm_pull(x, s1, r, g, width):
    dot = jnp.sum(g * x, axis=-1, keepdims=True)
    return g * r - (r * r * r * dot / width) * (x + s1)


def widen(ref, scratch):
    rows, width = ref.shape
    wide = scratch.shape[1]
    scratch[:, wide - LANES :] = jnp.zeros((rows, LANES), F32)
    scratch[:, :width] = ref[...].astype(F32)


def diag_mask(first, rows, live, turned):
    q_dim, k_dim = (1, 0) if turned else (0, 1)
    q = lax.broadcasted_iota(jnp.int32, (rows, rows), q_dim)
    k = lax.broadcasted_iota(jnp.int32, (rows, rows), k_dim)
    seen = (k <= q) & ((k + first < live) | (k == q))
    return jnp.where(seen, 0.0, HIDE).astype(F32)


def attend_kernel(seq_ref, live_ref, n1_ref, w_ref, b_ref, qx_ref, kx_ref, vx_ref, o_ref, pack_ref, mask_ref, s_ref):
    blocks, rows = pack_ref.shape[0], n1_ref.shape[0] // pack_ref.shape[0]
    seq, live = seq_ref[0], live_ref[0]
    lane = lane_ids(rows)
    low = lane < HEAD
    row = lax.broadcasted_iota(jnp.int32, (rows, LANES), 0)

    def project(i, carry):
        at = pl.ds(pl.multiple_of(i * rows, rows), rows)
        qkv = nn(n1_ref[at, :], w_ref[...]) + b_ref[...]
        qkv = qkv.astype(BF).astype(F32)
        key = row + i * rows
        m = lane - HEAD
        same = ((m * rows) ^ (i * rows)) < seq
        open_ = (m == i) | (same & (key < live))
        bias = jnp.where(m < blocks, jnp.where(open_, 0.0, HIDE), jnp.where(m < blocks + 3, 1.0, 0.0))
        hot = jnp.where(m == i, 1.0, 0.0)
        ones = jnp.where(m < 3, 1.0, 0.0)
        for h in range(3):
            pair = qkv[:, h * LANES : (h + 1) * LANES]
            qx_ref[h, at, :] = jnp.where(low, pair * HEAD**-0.5, hot).astype(BF)
            kx_ref[h, at, :] = jnp.where(low, half_turn(pair), bias).astype(BF)
            val = qkv[:, (3 + h // 2) * LANES : (4 + h // 2) * LANES]
            vx_ref[h, at, :] = jnp.where(low, half_turn(val) if h % 2 else val, ones).astype(BF)
        mask_ref[i] = diag_mask(i * rows, rows, live, False)
        return carry

    lax.fori_loop(0, blocks, project, 0)

    def head(h, carry):
        for i in range(blocks):
            q = qx_ref[h, i * rows : (i + 1) * rows, :]
            top = None
            for j in range(i, -1, -1):
                s = nt(q, kx_ref[h, j * rows : (j + 1) * rows, :])
                if i == j:
                    s = s + mask_ref[i]
                peak = jnp.max(s, axis=-1, keepdims=True)
                top = peak if top is None else jnp.maximum(top, peak)
                s_ref[j] = s
            acc = None
            for j in range(i + 1):
                p = jnp.exp(s_ref[j] - top).astype(BF)
                part = nn(p, vx_ref[h, j * rows : (j + 1) * rows, :])
                acc = part if acc is None else acc + part
            mass = acc[:, HEAD : HEAD + 1]
            lse = top + jnp.log(mass)
            o_ref[h, i * rows : (i + 1) * rows, :] = acc / mass
            hi, mid, lo = split3(-lse)
            ext = jnp.where(
                lane == HEAD + blocks,
                hi,
                jnp.where(lane == HEAD + blocks + 1, mid, jnp.where(lane == HEAD + blocks + 2, lo, q.astype(F32))),
            )
            qx_ref[h, i * rows : (i + 1) * rows, :] = ext.astype(BF)
        return carry

    lax.fori_loop(0, 3, head, 0)

    def pack(i, carry):
        at = pl.ds(pl.multiple_of(i * rows, rows), rows)
        pack_ref[i, :rows, :] = jnp.where(low, o_ref[0, at, :], half_turn(o_ref[1, at, :])).astype(BF)
        pack_ref[i, rows:, :] = fold(o_ref[2, at, :]).astype(BF)
        return carry

    lax.fori_loop(0, blocks, pack, 0)


def attend(seq, live, n1, w, b, blocks):
    total = n1.shape[0]
    rows = total // blocks
    ext = jax.ShapeDtypeStruct((3, total, LANES), BF)
    return pl.pallas_call(
        attend_kernel,
        out_shape=(
            ext,
            ext,
            ext,
            jax.ShapeDtypeStruct((3, total, LANES), F32),
            jax.ShapeDtypeStruct((blocks, rows + rows // 2, LANES), BF),
        ),
        in_specs=[SMEM, SMEM, VMEM, VMEM, VMEM],
        out_specs=(VMEM,) * 5,
        scratch_shapes=[pltpu.VMEM((blocks, rows, rows), F32), pltpu.VMEM((blocks, rows, rows), F32)],
        compiler_params=pltpu.CompilerParams(vmem_limit_bytes=LIMIT),
    )(seq, live, n1, w, b)


def middle_kernel(
    width, heads_ref, tok_ref, cot_ref, full_ref, ob_ref, db_ref,
    mixed_ref, hid_ref, hg_ref, grad_ref,
    wu, wd, wm, wb, wo, wide, xall, n2_ref, gb_ref, dn_ref, sem,
):
    parts, rows = heads_ref.shape[0], tok_ref.shape[0]
    nd, piece = wu.shape[1:3]
    unit = piece * nd
    tail = grad_ref.shape[2] - 2 * piece

    def fetch(t, k):
        if k == 3:
            source = full_ref.at[0, t, pl.ds(3 * piece, 16), :]
        else:
            source = full_ref.at[:, t, pl.ds(k * piece, piece), :]
        return pltpu.make_async_copy(source, (wu, wd, wm, wb)[k].at[t], sem.at[t, k])

    for k in (2, 0, 1, 3):
        for t in range(parts):
            fetch(t, k).start()
    low = lane_ids(rows) < HEAD
    lows = []
    for t in range(parts):
        xall[:, t * LANES : (t + 1) * LANES] = heads_ref[t, :rows, :]
        lows.append(unfold(heads_ref[t, rows:, :].astype(F32)))
    for k in range(parts // 2):
        both = jnp.where(low, lows[2 * k], half_turn(lows[2 * k + 1]))
        xall[:, (parts + k) * LANES : (parts + k + 1) * LANES] = both.astype(BF)
    for t in range(parts):
        fetch(t, 2).wait()
        own = wm[t].reshape(unit, unit)
        wo[t * LANES : (t + 1) * LANES, :] = own[:LANES]
        wo[parts * LANES + t * HEAD : parts * LANES + (t + 1) * HEAD, :] = own[LANES : LANES + HEAD]
    widen(tok_ref, wide)
    hidden = wide[...] + nn(xall[...], wo[...]) + ob_ref[...]
    s1, r = norm_stats(hidden, width + 1)
    n2_ref[...] = (hidden * r).astype(BF)
    hid_ref[...] = hidden
    widen(cot_ref, wide)
    gb_ref[...] = wide[...].astype(BF)
    wide[...] = hidden + db_ref[...]
    dn_ref[...] = jnp.zeros_like(dn_ref)
    root = (2 / jnp.pi) ** 0.5

    def unit_block(t, carry):
        for k in (0, 1, 3):
            fetch(t, k).wait()
        up = wu[t].reshape(unit, unit)
        down = wd[t].reshape(unit, unit)
        u = nn(n2_ref[...], up) + wb[t].astype(F32)[:1]
        th = jnp.tanh(root * (u + 0.044715 * (u * u * u)))
        act = (0.5 * u * (1 + th)).astype(BF)
        slope = 0.5 * (1 + th) + (0.5 * u) * (1 - th * th) * (root * (1 + 0.134145 * (u * u)))
        wide[...] += nn(act, down)
        ug32 = nt(gb_ref[...], down) * slope
        ug = ug32.astype(BF)
        dn_ref[...] += nt(ug, up)
        bias_grad = jnp.sum(ug.astype(F32), axis=0, keepdims=True)
        grad_ref[:, t, :piece, :] = tn(n2_ref[...], ug).astype(BF).reshape(nd, piece, unit)
        grad_ref[:, t, piece : 2 * piece, :] = tn(act, gb_ref[...]).astype(BF).reshape(nd, piece, unit)
        grad_ref[nd - 1, t, 2 * piece :, :] = jnp.broadcast_to(bias_grad, (tail, unit)).astype(BF)
        return carry

    lax.fori_loop(0, parts, unit_block, 0)
    mixed_ref[...] = wide[:, :width].astype(BF)
    hidden = hid_ref[...]
    gout = gb_ref[...].astype(F32)
    down_bias_grad = jnp.sum(gout, axis=0, keepdims=True)
    hidgrad = gout + norm_pull(hidden, s1, r, dn_ref[...], width + 1)
    hid_ref[...] = hidgrad
    out_bias_grad = jnp.sum(hidgrad, axis=0, keepdims=True)
    ag = hidgrad.astype(BF)
    hg = nt(ag, wo[...])
    for t in range(parts):
        hg_ref[t, :rows, :] = hg[:, t * LANES : (t + 1) * LANES].astype(BF)
        pair = hg[:, (parts + t // 2) * LANES : (parts + t // 2 + 1) * LANES]
        hg_ref[t, rows:, :] = fold(half_turn(pair) if t % 2 else pair).astype(BF)
    og = tn(xall[...], ag)
    last = tail * nd - (LANES + HEAD)
    spot = lax.broadcasted_iota(jnp.int32, (last, unit), 0)
    for t in range(parts):
        ubg = grad_ref[nd - 1, t, 2 * piece :, :].astype(F32)[:1]
        extra = jnp.where(
            spot == 0, ubg, jnp.where(spot == 1, out_bias_grad, jnp.where(spot == 2, down_bias_grad, 0.0))
        )
        own = jnp.concatenate(
            [og[t * LANES : (t + 1) * LANES], og[parts * LANES + t * HEAD : parts * LANES + (t + 1) * HEAD], extra],
            axis=0,
        )
        grad_ref[:, t, 2 * piece :, :] = own.astype(BF).reshape(nd, tail, unit)


def middle(heads, tokens, cotangent, full, out_bias, down_bias):
    parts, nd = heads.shape[0], full.shape[0]
    rows, width = tokens.shape
    unit = full.shape[-1]
    piece = unit // nd
    tail = 256 // nd
    weight = pltpu.VMEM((parts, nd, piece, unit), BF)
    square = pltpu.VMEM((rows, unit), F32)
    half = pltpu.VMEM((rows, unit), BF)
    return pl.pallas_call(
        partial(middle_kernel, width),
        out_shape=(
            jax.ShapeDtypeStruct((rows, width), BF),
            jax.ShapeDtypeStruct((rows, unit), F32),
            jax.ShapeDtypeStruct(heads.shape, BF),
            jax.ShapeDtypeStruct((nd, parts, 2 * piece + tail, unit), BF),
        ),
        in_specs=[VMEM, VMEM, VMEM, ANY, VMEM, VMEM],
        out_specs=(VMEM,) * 4,
        scratch_shapes=[
            weight, weight, weight,
            pltpu.VMEM((parts, 16, unit), BF),
            pltpu.VMEM((unit, unit), BF),
            square, half, half, half, square,
            pltpu.SemaphoreType.DMA((parts, 4)),
        ],
        compiler_params=pltpu.CompilerParams(vmem_limit_bytes=LIMIT),
    )(heads, tokens, cotangent, full, out_bias, down_bias)


def attend_back_kernel(
    live_ref, n1_ref, qx_ref, kx_ref, vx_ref, o_ref, hg_ref, pack_ref, wg_ref, dox, grads, dqt, dk_ref, mask_ref
):
    blocks, rows = hg_ref.shape[0], n1_ref.shape[0] // hg_ref.shape[0]
    live = live_ref[0]
    lane = lane_ids(rows)
    low = lane < HEAD

    def extend(i, carry):
        at = pl.ds(pl.multiple_of(i * rows, rows), rows)
        pair = hg_ref[i, :rows, :].astype(F32)
        third = unfold(hg_ref[i, rows:, :].astype(F32))
        for h, g in enumerate((pair, half_turn(pair), third)):
            g = jnp.where(low, g, 0.0)
            hi, mid, lo = split3(-jnp.sum(g * o_ref[h, at, :], axis=-1, keepdims=True))
            g = jnp.where(lane == HEAD, hi, jnp.where(lane == HEAD + 1, mid, jnp.where(lane == HEAD + 2, lo, g)))
            dox[h, at, :] = g.astype(BF)
        mask_ref[i] = diag_mask(i * rows, rows, live, True)
        return carry

    lax.fori_loop(0, blocks, extend, 0)

    def head(h, carry):
        for j in range(blocks):
            keys = kx_ref[h, j * rows : (j + 1) * rows, :]
            keys_t = jnp.transpose(keys.astype(F32)).astype(BF)
            vals = vx_ref[h, j * rows : (j + 1) * rows, :]
            dk = dv = None
            for i in range(j, blocks):
                q = qx_ref[h, i * rows : (i + 1) * rows, :]
                do = dox[h, i * rows : (i + 1) * rows, :]
                s = nt(keys, q)
                if i == j:
                    s = s + mask_ref[i]
                p = jnp.exp(s)
                ds = (p * nt(vals, do)).astype(BF)
                dv_part = nn(p.astype(BF), do)
                dk_part = nn(ds, q)
                dq_part = nn(keys_t, ds)
                dk = dk_part if dk is None else dk + dk_part
                dv = dv_part if dv is None else dv + dv_part
                if j == 0:
                    dqt[i] = dq_part
                else:
                    dqt[i] += dq_part
            dk_ref[j] = dk
            grads[3 + h, j * rows : (j + 1) * rows, :] = jnp.where(low, dv, 0.0)
        for i in range(blocks):
            dq = jnp.transpose(dqt[i]) * HEAD**-0.5
            grads[h, i * rows : (i + 1) * rows, :] = jnp.where(low, dq, half_turn(dk_ref[i]))
        return carry

    lax.fori_loop(0, 3, head, 0)

    def pack(i, carry):
        at = pl.ds(pl.multiple_of(i * rows, rows), rows)
        for h in range(3):
            pack_ref[i, h * rows : (h + 1) * rows, :] = grads[h, at, :].astype(BF)
        both = jnp.where(low, grads[3, at, :], half_turn(grads[4, at, :]))
        grads[3, at, :] = both
        pack_ref[i, 3 * rows : 4 * rows, :] = both.astype(BF)
        pack_ref[i, 4 * rows :, :] = fold(grads[5, at, :]).astype(BF)
        return carry

    lax.fori_loop(0, blocks, pack, 0)
    spot = lax.broadcasted_iota(jnp.int32, (n1_ref.shape[1], LANES), 0)
    for k, m in enumerate((0, 1, 2, 3, 5)):
        g = grads[m].astype(BF)
        tall = jnp.sum(g.astype(F32), axis=0, keepdims=True)
        wg_ref[:, k * LANES : (k + 1) * LANES] = jnp.where(
            spot == n1_ref.shape[1] - 1, tall, tn(n1_ref[...], g)
        )


def attend_back(live, n1, qx, kx, vx, o, hg):
    blocks = hg.shape[0]
    total, unit = n1.shape
    rows = total // blocks
    return pl.pallas_call(
        attend_back_kernel,
        out_shape=(
            jax.ShapeDtypeStruct((blocks, 4 * rows + rows // 2, LANES), BF),
            jax.ShapeDtypeStruct((unit, 5 * LANES), F32),
        ),
        in_specs=[SMEM] + [VMEM] * 6,
        out_specs=(VMEM, VMEM),
        scratch_shapes=[
            pltpu.VMEM((3, total, LANES), BF),
            pltpu.VMEM((6, total, LANES), F32),
            pltpu.VMEM((blocks, LANES, rows), F32),
            pltpu.VMEM((blocks, rows, LANES), F32),
            pltpu.VMEM((blocks, rows, rows), F32),
        ],
        compiler_params=pltpu.CompilerParams(vmem_limit_bytes=LIMIT),
    )(live, n1, qx, kx, vx, o, hg)


def final_kernel(width, tok_ref, hid_ref, pack_ref, full_ref, out_ref, wm, wide, dn_ref, xt, sem):
    parts, rows = pack_ref.shape[0], tok_ref.shape[0]
    nd, piece = wm.shape[1:3]
    unit = piece * nd
    for t in range(parts):
        pltpu.make_async_copy(full_ref.at[:, t, pl.ds(2 * piece, piece), :], wm.at[t], sem.at[t]).start()
    widen(tok_ref, wide)
    dn_ref[...] = jnp.zeros_like(dn_ref)

    def part(t, carry):
        pltpu.make_async_copy(full_ref.at[:, t, pl.ds(2 * piece, piece), :], wm.at[t], sem.at[t]).wait()
        w = wm[t].reshape(unit, unit)[LANES + HEAD :]
        for k in range(4):
            xt[:, k * LANES : (k + 1) * LANES] = pack_ref[t, k * rows : (k + 1) * rows, :]
        xt[:, 4 * LANES :] = unfold(pack_ref[t, 4 * rows :, :].astype(F32)).astype(BF)
        dn_ref[...] += nn(xt[:, : 9 * HEAD], w)
        return carry

    lax.fori_loop(0, parts, part, 0)
    x = wide[...]
    s1, r = norm_stats(x, width + 1)
    grad = hid_ref[...] + norm_pull(x, s1, r, dn_ref[...], width + 1)
    out_ref[...] = grad[:, :width].astype(BF)


def final(tokens, hidgrad, pack, full):
    parts, nd = pack.shape[0], full.shape[0]
    rows, width = tokens.shape
    unit = full.shape[-1]
    return pl.pallas_call(
        partial(final_kernel, width),
        out_shape=jax.ShapeDtypeStruct((rows, width), BF),
        in_specs=[VMEM, VMEM, VMEM, ANY],
        out_specs=VMEM,
        scratch_shapes=[
            pltpu.VMEM((parts, nd, unit // nd, unit), BF),
            pltpu.VMEM((rows, unit), F32),
            pltpu.VMEM((rows, unit), F32),
            pltpu.VMEM((rows, 5 * LANES), BF),
            pltpu.SemaphoreType.DMA((parts,)),
        ],
        compiler_params=pltpu.CompilerParams(vmem_limit_bytes=LIMIT),
    )(tokens, hidgrad, pack, full)


def swap(x):
    return lax.all_to_all(x, "tensor", 0, 0, tiled=True)


def pair_order(w):
    w = w.reshape(w.shape[:-1] + (3, HEAD))
    front = jnp.swapaxes(w[..., :2, :, :], -3, -2)
    lead = w.shape[:-3]
    return jnp.concatenate([front.reshape(lead + (6 * HEAD,)), w[..., 2, :, :].reshape(lead + (3 * HEAD,))], axis=-1)


def pair_disorder(g):
    lead = g.shape[:-1]
    front = jnp.swapaxes(g[..., : 6 * HEAD].reshape(lead + (3, 2, HEAD)), -3, -2)
    return jnp.concatenate([front, g[..., 6 * HEAD :].reshape(lead + (1, 3, HEAD))], axis=-3).reshape(
        lead + (3, 3 * HEAD)
    )


def local(
    groups,
    tokens,
    cotangent,
    seq_length,
    live_rows,
    qkv_weight,
    qv_bias,
    out_weight,
    out_bias,
    up_weight,
    up_bias,
    down_weight,
    down_bias,
):
    parts = groups["tensor"]
    nd = 8 if groups["dp"] == 8 else 1
    rows, width = tokens.shape
    unit = width + 1
    piece = unit // nd
    tail = 256 // nd
    me = lax.axis_index("dp") * piece if nd > 1 else 0

    wide_in = jnp.pad(tokens.astype(F32), ((0, 0), (0, 1)))
    s1, r = norm_stats(wide_in, unit)
    n1 = lax.all_gather((wide_in * r).astype(BF), "tensor", axis=0, tiled=True)

    qkv_flat = pair_order(qkv_weight)
    def rows_of(w):
        return lax.dynamic_slice_in_dim(w, me, piece, 0)

    up_rows = rows_of(jnp.pad(up_weight, ((0, 1), (0, 0))))
    down_rows = jnp.pad(rows_of(down_weight), ((0, 0), (0, 1)))
    misc = jnp.pad(jnp.concatenate([out_weight, qkv_flat.T], axis=0), ((0, 0), (0, 1)))
    bias_rows = jnp.broadcast_to(up_bias[None], (16, unit))
    full = lax.all_gather(
        jnp.concatenate([up_rows, down_rows, rows_of(misc), bias_rows], axis=0),
        BOTH if nd > 1 else "tensor",
        axis=0,
        tiled=False,
    ).reshape(nd, parts, 3 * piece + 16, unit)

    w = jnp.pad(qkv_flat, ((0, 1), (0, HEAD)))
    zero = jnp.zeros_like(qv_bias[0])
    b = jnp.pad(pair_order(jnp.stack([qv_bias[0], zero, qv_bias[1]])), (0, HEAD)).astype(F32)[None]
    qx, kx, vx, o, heads = attend(seq_length, live_rows, n1, w, b, parts)
    heads = swap(heads)
    as_row = lambda v: jnp.pad(v.astype(F32), (0, 1))[None]
    mixed, hidgrad, hg, grads = middle(heads, tokens, cotangent, full, as_row(out_bias), as_row(down_bias))
    if nd > 1:
        mine = lax.psum_scatter(grads, "dp", scatter_dimension=0, tiled=False)
        mine = lax.psum_scatter(mine, "tensor", scatter_dimension=0, tiled=False)
        mine = lax.all_gather(mine, "dp", axis=0, tiled=False)
    else:
        mine = lax.psum_scatter(grads[0].astype(F32), "tensor", scatter_dimension=0, tiled=False)
        mine = lax.psum(mine, "dp")[None]
    pack, wg = attend_back(live_rows, n1, qx, kx, vx, o, swap(hg))
    token_grad = final(tokens, hidgrad, swap(pack), full)
    wg = lax.psum(wg, "dp")
    up_grad = mine[:, :piece].reshape(unit, unit)[:width].astype(F32)
    down_grad = mine[:, piece : 2 * piece].reshape(unit, unit)[:, :width].astype(F32)
    rest = mine[:, 2 * piece :].reshape(256, unit).astype(F32)
    out_grad = rest[: 3 * HEAD, :width]
    wg = pair_disorder(wg[:, : 9 * HEAD])
    return (
        mixed,
        token_grad,
        wg[:width],
        jnp.stack([wg[width, 0], wg[width, 2]]),
        out_grad,
        rest[3 * HEAD + 1, :width],
        up_grad,
        rest[3 * HEAD],
        down_grad,
        rest[3 * HEAD + 2, :width],
    )


def solution(mesh):
    placed = (
        P(BOTH, None),
        P(BOTH, None),
        P("dp"),
        P("dp"),
        P(None, None, "tensor"),
        P(None, "tensor"),
        P("tensor", None),
        P(),
        P(None, "tensor"),
        P("tensor"),
        P("tensor", None),
        P(),
    )
    return jax.shard_map(
        partial(local, dict(mesh.shape)),
        mesh=mesh,
        in_specs=placed,
        out_specs=(
            P(BOTH, None),
            P(BOTH, None),
            P(None, None, "tensor"),
            P(None, "tensor"),
            P("tensor", None),
            P(),
            P(None, "tensor"),
            P("tensor"),
            P("tensor", None),
            P(),
        ),
        check_vma=False,
    )
```

time: 1130 us -> 493 us (0.44); the launches traced: 1120 us -> 492 us
  waiting for transfers between devices: 765 us -> 297 us
  matrix products: 151 us -> 0 us
  Pallas kernels: 0 us -> 95.7 us
  blocking collectives: 105 us -> 43.5 us
  other arithmetic: 42.4 us -> 9.83 us
    reduce_scatter x4 -> x2, waiting for transfers between devices: 421 us -> 82.3 us  [the longest x1 82.3 us: local(): mine = lax.psum_scatter(grads, 'dp', scatter_dimension=0, tiled=False)]
    dot_general x49 -> x0, matrix products: 151 us -> none  [the longest x5 18.3 us: out_update(): jnp.einsum('hqk,khd->qhd', softmaxed, value_rows.astype(jnp.float32), pre...]
    all_gather x4 -> x3, waiting for transfers between devices: 229 us -> 124 us  [the longest x1 56.3 us: local(): n1 = lax.all_gather((wide_in * r).astype(BF), 'tensor', axis=0, tiled=True)]
    psum x2 -> x0, blocking collectives: 105 us -> none  [the longest x1 90.2 us: local(): lax.psum((jnp.sum(hidden_grad, axis=0), jnp.sum(grad_out, axis=0)), ('dp'...]
    pallas_call x0 -> x4, Pallas kernels: none -> 95.7 us  [the longest x1 33.4 us: attend_back(): pl.pallas_call(attend_back_kernel, out_shape=(jax.ShapeDtypeStruct((block...]
    psum x1, waiting for transfers between devices: 115 us -> 54.4 us  [local(): wg = lax.psum(wg, 'dp')]
    all_to_all x0 -> x1, blocking collectives: none -> 43.5 us  [swap(): return lax.all_to_all(x, 'tensor', 0, 0, tiled=True)]
    all_to_all x0 -> x2, waiting for transfers between devices: none -> 36.5 us  [swap(): return lax.all_to_all(x, 'tensor', 0, 0, tiled=True)]
  transfers between devices with their start and end apart: 9 -> 8, of which waited for: 9 -> 6; matrix products, arithmetic and copies ran while one was open for 5% -> 3% of each run, Pallas kernels for 0% -> 13%
where the time goes in v1:
time: 493 us; the launch traced here: 492 us
  waiting for transfers between devices  297 us (60%)
  Pallas kernels  95.7 us (19%)
  blocking collectives  43.5 us (9%)
  local copies, waits for them, and re-layouts  22.3 us (5%)
  between operations  15.7 us (3%)
  other arithmetic  9.83 us (2%)
  starting transfers between devices  7.98 us (2%)
    reduce_scatter x1, waiting for transfers between devices, local(): mine = lax.psum_scatter(grads, 'dp', scatter_dimension=0, tiled=False)  82.3 us
    all_gather x1, waiting for transfers between devices, local(): n1 = lax.all_gather((wide_in * r).astype(BF), 'tensor', axis=0, tiled=True)  56.3 us
    all_gather x1, waiting for transfers between devices, local(): lax.all_gather(jnp.concatenate([up_rows, down_rows, rows_of(misc), bias_r...  55.7 us
    psum x1, waiting for transfers between devices, local(): wg = lax.psum(wg, 'dp')  54.4 us
    all_to_all x1, blocking collectives, swap(): return lax.all_to_all(x, 'tensor', 0, 0, tiled=True)  43.5 us
    all_to_all x2, waiting for transfers between devices, swap(): return lax.all_to_all(x, 'tensor', 0, 0, tiled=True)  36.5 us
    pallas_call x1, Pallas kernels, attend_back(): pl.pallas_call(attend_back_kernel, out_shape=(jax.ShapeDtypeStruct((block...  33.4 us
    pallas_call x1, Pallas kernels, middle(): pl.pallas_call(partial(middle_kernel, width), out_shape=(jax.ShapeDtypeSt...  30.2 us
  transfers between devices with their start and end apart: 8, of which 6 were waited for; matrix products, arithmetic and copies ran while one was open for 3% of the time, Pallas kernels for 13%

profile of v1, /device:TPU:0, one launch (start us, length us, event | category | flops | bytes accessed | tf_op | source)
XLA Modules:
  0.0 492.3 jit_solution(17950666947337976590)
XLA Ops:
  7.2 1.5 convert_reduce_fusion
  8.8 2.3 fusion.1
  11.4 0.9 copy.56
  12.9 1.6 copy.58
  14.5 1.2 fusion.14
  16.9 1.0 copy.61
  20.1 1.0 pad.39.w_ref
  21.2 56.3 %all-gather.5.cloned.1.call-done.n1_ref = bf16[2048,768]{1,0:T(8,128)(2,1)} async-done(((bf16[512,768]{1,0:T(8,128)(2,1)}), bf16[2048,768]{1,0:T(8,128)(2,1)}) %all-gather.5.cloned.1.call-update) | async-done | bytes 3145744 | tf_op jit(solution)/shard_map/all_gather | solution.py:485
  77.5 23.7 %shard_map.195 = (bf16[3,2048,128]{2,1,0:T(8,128)(2,1)}, bf16[3,2048,128]{2,1,0:T(8,128)(2,1)}, bf16[3,2048,128]{2,1,0:T(8,128)(2,1)}, f32[3,2048,128]{2,1,0:T(8,128)}, bf16[4,768,128]{2,1,0:T(8,128)(2,1)}) custom-call(s32[1]{0:T(128)S(6)} %copy.69.seq_ref, s32[1]{0:T(128)S(6)} %copy.70.live_ref, bf16[2048,768]{1,0:T(8,128)(2,1)} %all-gather.5.cloned.1.call-done.n1_ref, ...), custom_call_target="tpu_custom_call" | custom-call | tf_op jit(solution)/shard_map/pallas_call | solution.py:161
  101.2 3.6 all-to-all-start
  106.3 36.5 %all-to-all-done.heads_ref = bf16[4,768,128]{2,1,0:T(8,128)(2,1)S(1)} async-done(((bf16[4,768,128]{2,1,0:T(8,128)(2,1)}), bf16[4,768,128]{2,1,0:T(8,128)(2,1)S(1)}, u32[]{:S(2)}, u32[]{:S(2)}) %all-to-all-start) | async-done | bytes 786464 | tf_op jit(solution)/shard_map/all_to_all | solution.py:442
  142.8 55.7 %all-gather.9.cloned.1.call-done = bf16[9728,768]{1,0:T(8,128)(2,1)} async-done(((bf16[304,768]{1,0:T(8,128)(2,1)}), bf16[9728,768]{1,0:T(8,128)(2,1)}) %all-gather.9.cloned.1.call-update) | async-done | bytes 14942224 | tf_op jit(solution)/shard_map/all_gather | solution.py:495
  198.4 30.2 %shard_map.196 = (bf16[512,767]{1,0:T(8,128)(2,1)}, f32[512,768]{1,0:T(8,128)}, bf16[4,768,128]{2,1,0:T(8,128)(2,1)}, bf16[8,4,224,768]{3,2,1,0:T(8,128)(2,1)}) custom-call(bf16[4,768,128]{2,1,0:T(8,128)(2,1)} %copy-done.3, bf16[512,767]{1,0:T(8,128)(2,1)} %tok_ref.3, bf16[512,767]{1,0:T(8,128)(2,1)} %cot_ref.1, bf16[8,4,304,768]{3,2,1,0:T(8,128)(2,1)} %bitcast.24, ...), custom_call_target="tpu_custom_call" | custom-call | tf_op jit(solution)/shard_map/pallas_call | solution.py:278
  228.7 82.3 %reduce-scatter.3.cloned.1.call-done = bf16[1,4,224,768]{3,2,1,0:T(8,128)(2,1)} async-done(((bf16[8,4,224,768]{3,2,1,0:T(8,128)(2,1)}), bf16[1,4,224,768]{3,2,1,0:T(8,128)(2,1)}) %reduce-scatter.3.cloned.1.call-update) | async-done | bytes 1376272 | tf_op jit(solution)/shard_map/reduce_scatter | solution.py:510
  311.1 43.5 %all_to_all.15.hg_ref = bf16[4,768,128]{2,1,0:T(8,128)(2,1)} all-to-all(bf16[4,768,128]{2,1,0:T(8,128)(2,1)S(1)} %copy-done.8), channel_id=1, replica_groups=mesh['dp'=8,'tensor'=4] {'tensor'}, dimensions={0} | all-to-all | bytes 1572864 | tf_op jit(solution)/shard_map/all_to_all | solution.py:442
  354.6 33.4 %shard_map.197 = (bf16[4,2304,128]{2,1,0:T(8,128)(2,1)}, f32[768,640]{1,0:T(8,128)}) custom-call(s32[1]{0:T(128)S(6)} %copy.70.live_ref, bf16[2048,768]{1,0:T(8,128)(2,1)} %all-gather.5.cloned.1.call-done.n1_ref, bf16[3,2048,128]{2,1,0:T(8,128)(2,1)} %get-tuple-element.24.qx_ref, bf16[3,2048,128]{2,1,0:T(8,128)(2,1)} %get-tuple-element.25.kx_ref, ...), custom_call_target="tpu_custom_call" | custom-call | tf_op jit(solution)/shard_map/pallas_call | solution.py:377
  388.6 3.9 all-to-all-start.2
  392.5 54.4 %all-reduce.10.cloned.1.call-done = f32[768,640]{1,0:T(8,128)} async-done(((f32[768,640]{1,0:T(8,128)}), f32[768,640]{1,0:T(8,128)}) %all-reduce.10.cloned.1.call-update) | async-done | bytes 1966096 | tf_op jit(solution)/shard_map/psum | solution.py:518
  446.9 1.1 slice-done
  448.1 1.1 copy.63
  449.1 2.4 slice.91
  451.5 1.6 copy.62
  453.2 1.0 copy-done.6
  454.3 1.3 copy.65
  455.6 0.9 copy-done.4
  457.3 1.4 copy-done.2
  458.7 8.4 %shard_map.198 = bf16[512,767]{1,0:T(8,128)(2,1)} custom-call(bf16[512,767]{1,0:T(8,128)(2,1)} %tok_ref.3, f32[512,768]{1,0:T(8,128)} %get-tuple-element.23.hid_ref, bf16[4,2304,128]{2,1,0:T(8,128)(2,1)} %copy-done.2, bf16[8,4,304,768]{3,2,1,0:T(8,128)(2,1)} %bitcast.25), custom_call_target="tpu_custom_call" | custom-call | tf_op jit(solution)/shard_map/pallas_call | solution.py:425
  467.1 11.6 %all-gather.7.cloned.1.call-done = bf16[8,224,768]{2,1,0:T(8,128)(2,1)} async-done(((bf16[1,224,768]{2,1,0:T(8,128)(2,1)}), bf16[8,224,768]{2,1,0:T(8,128)(2,1)}) %all-gather.7.cloned.1.call-update) | async-done | bytes 2752528 | tf_op jit(solution)/shard_map/all_gather | solution.py:512
  478.7 1.2 slice.95
  481.2 0.9 slice.96
  482.2 1.6 slice_convert_fusion.1
  483.8 1.6 slice_convert_fusion
  (73 shorter events, 7.7 us)
Async XLA Ops:
  7.2 4.0 copy-start
  7.2 70.3 %all-gather.5.cloned.1.call-start = ((), (), s32[]{:S(2)}) async-start(), calls=%async_computation.5 | async-start | bytes 3932160 | tf_op jit(solution)/shard_map/all_gather | solution.py:485
  8.8 2.6 copy-start.7
  11.1 1.2 copy-start.9
  11.1 187.3 %all-gather.9.cloned.1.call-start = ((), (), s32[]{:S(2)}) async-start(), calls=%async_computation.10 | async-start | bytes 15409152 | tf_op jit(solution)/shard_map/all_gather | solution.py:495
  15.6 0.7 copy-start.10
  16.5 2.8 copy-start.13
  16.5 2.8 copy-start.14
  101.2 3.9 copy-start.11
  101.2 4.5 copy-start.12
  101.2 41.5 %all-to-all-start = ((bf16[4,768,128]{2,1,0:T(8,128)(2,1)}), bf16[4,768,128]{2,1,0:T(8,128)(2,1)S(1)}, u32[]{:S(2)}, u32[]{:S(2)}) async-start(bf16[4,768,128]{2,1,0:T(8,128)(2,1)} %get-tuple-element.21), calls=%async_computation | async-start | bytes 1572864 | tf_op jit(solution)/shard_map/all_to_all | solution.py:442
  104.9 206.2 %reduce-scatter.3.cloned.1.call-start = ((), (), s32[]{:S(2)}) async-start(), calls=%async_computation.7 | async-start | bytes 12386304 | tf_op jit(solution)/shard_map/reduce_scatter | solution.py:510
  142.8 55.7 %copy-start.3 = (bf16[4,768,128]{2,1,0:T(8,128)(2,1)}, bf16[4,768,128]{2,1,0:T(8,128)(2,1)S(1)}, u32[]{:S(2)}) copy-start(bf16[4,768,128]{2,1,0:T(8,128)(2,1)S(1)} %all-to-all-done.heads_ref) | copy-start | bytes 2359300
  228.7 82.4 %copy-start.8 = (bf16[4,768,128]{2,1,0:T(8,128)(2,1)S(1)}, bf16[4,768,128]{2,1,0:T(8,128)(2,1)}, u32[]{:S(2)}) copy-start(bf16[4,768,128]{2,1,0:T(8,128)(2,1)} %get-tuple-element.28) | copy-start | bytes 2359300
  228.7 159.4 %reduce-scatter.5.cloned.1.call-start = ((), (), s32[]{:S(2)}) async-start(), calls=%async_computation.8 | async-start | bytes 1720320 | tf_op jit(solution)/shard_map/reduce_scatter | solution.py:511
  311.0 135.9 %all-reduce.10.cloned.1.call-start = ((), (), s32[]{:S(2)}) async-start(), calls=%async_computation.6 | async-start | bytes 3932160 | tf_op jit(solution)/shard_map/psum | solution.py:518
  388.0 90.7 %all-gather.7.cloned.1.call-start = ((), (), s32[]{:S(2)}) async-start(), calls=%async_computation.9 | async-start | bytes 3096576 | tf_op jit(solution)/shard_map/all_gather | solution.py:512
  388.6 68.8 %all-to-all-start.2 = ((bf16[4,2304,128]{2,1,0:T(8,128)(2,1)}), bf16[4,2304,128]{2,1,0:T(8,128)(2,1)S(1)}, u32[]{:S(2)}, u32[]{:S(2)}) async-start(bf16[4,2304,128]{2,1,0:T(8,128)(2,1)} %get-tuple-element.29), calls=%async_computation.2 | async-start | bytes 4718592 | tf_op jit(solution)/shard_map/all_to_all | solution.py:442
  446.9 1.1 slice-start
  453.1 1.1 copy-start.6
  454.3 2.2 copy-start.4
  457.3 1.4 copy-start.2
  478.7 3.3 copy-start.5
  483.8 1.7 copy-start.1
Sparse Core Ops, SparseCore 0:
  11.2 66.2 all-gather.4
  80.9 117.5 all-gather.8
  228.8 82.1 reduce-scatter.2
  313.2 44.3 reduce-scatter.4
  388.1 58.7 all-reduce.9
  448.8 29.8 all-gather.6

commit v2 on v1

--- a/solution.py
+++ b/solution.py
@@ -86,16 +86,213 @@
     return jnp.where(seen, 0.0, HIDE).astype(F32)
 
 
-def attend_kernel(seq_ref, live_ref, n1_ref, w_ref, b_ref, qx_ref, kx_ref, vx_ref, o_ref, pack_ref, mask_ref, s_ref):
-    blocks, rows = pack_ref.shape[0], n1_ref.shape[0] // pack_ref.shape[0]
+def at_rows(i, rows):
+    return pl.ds(pl.multiple_of(i * rows, rows), rows)
+
+
+def fill_rows(dst, src, first, rows, width):
+    wide = dst.shape[1]
+    dst[first : first + rows, wide - LANES :] = jnp.zeros((rows, LANES), dst.dtype)
+    dst[first : first + rows, :width] = src
+
+
+class Sends:
+    def __init__(self):
+        self.ends = []
+
+    def start(self, copy, when=None):
+        if when is None:
+            copy().start()
+        else:
+            pl.when(when())(lambda: copy().start())
+        self.ends.append((copy, when))
+
+    def finish(self):
+        for copy, when in self.ends:
+            if when is None:
+                copy().wait_send()
+            else:
+                pl.when(when())(lambda copy=copy: copy().wait_send())
+
+
+def remote(src, dst, ssem, rsem, **where):
+    return pltpu.make_async_remote_copy(
+        src_ref=src,
+        dst_ref=dst,
+        send_sem=ssem,
+        recv_sem=rsem,
+        device_id=where,
+        device_id_type=pl.DeviceIdType.MESH,
+    )
+
+
+def neighbours(d):
+    core, x, y = d % 2, (d // 2) % 2, d // 4
+    return d + 1 - 2 * core, d + 2 - 4 * x, d + 4 - 8 * y
+
+
+def greet(d, t, parts, spread):
+    barrier = pltpu.get_barrier_semaphore()
+
+    def signal(**where):
+        pl.semaphore_signal(barrier, inc=1, device_id=where, device_id_type=pl.DeviceIdType.MESH)
+
+    for k in range(1, parts):
+        signal(tensor=lax.rem(t + k, parts))
+    if spread:
+        for n in neighbours(d):
+            signal(dp=n)
+    return lambda: pl.semaphore_wait(barrier, parts - 1 + 3 * spread)
+
+
+class Spread:
+    def __init__(self, d, t, parts, piece, full, zsem, xsem, csem, sends):
+        self.d, self.t, self.parts, self.piece, self.full = d, t, parts, piece, full
+        self.zsem, self.xsem, self.csem, self.sends = zsem, xsem, csem, sends
+        self.core_n, self.x_n, self.y_n = neighbours(d)
+        self.diag = self.x_n + self.y_n - d
+
+    def slot(self, e, b):
+        return self.full.at[e, b]
+
+    def along(self, b, first, up, ok):
+        t, d = self.t, self.d
+        src = lambda: self.piece if first else self.slot(d, b)
+        k, step = (1, 1) if up else (2, -1)
+        edge = (lambda: t < self.parts - 1) if up else (lambda: t > 0)
+        self.sends.start(
+            lambda: remote(src(), self.slot(d, b), self.zsem.at[k, b], self.zsem.at[0, b], tensor=t + step),
+            lambda: ok() & edge(),
+        )
+
+    def plane(self, b, first, ok):
+        d, xs = self.d, self.xsem
+        src = lambda: self.piece if first else self.slot(d, b)
+        self.sends.start(lambda: remote(src(), self.slot(d, b), xs.at[0, b], xs.at[1, b], dp=self.x_n), ok)
+        self.sends.start(lambda: remote(src(), self.slot(d, b), xs.at[2, b], xs.at[3, b], dp=self.y_n), ok)
+        self.sends.start(
+            lambda: remote(src(), self.slot(d, b), self.csem.at[0, b], self.csem.at[4, b], dp=self.core_n), ok
+        )
+
+    def from_z(self, b, ok, up):
+        def wait():
+            remote(self.slot(self.d, b), self.slot(self.d, b), self.zsem.at[1, b], self.zsem.at[0, b], tensor=self.t).wait_recv()
+
+        pl.when(ok())(wait)
+        self.along(b, False, up, ok)
+        self.plane(b, False, ok)
+
+    def across(self, b, ok):
+        xs, cs = self.xsem, self.csem
+        east = lambda: self.slot(self.x_n, b)
+        north = lambda: self.slot(self.y_n, b)
+
+        def wait():
+            remote(east(), east(), xs.at[0, b], xs.at[1, b], dp=self.x_n).wait_recv()
+            remote(north(), north(), xs.at[2, b], xs.at[3, b], dp=self.y_n).wait_recv()
+
+        pl.when(ok())(wait)
+        self.sends.start(
+            lambda: remote(east(), east(), xs.at[4, b], xs.at[5, b], dp=self.y_n), lambda: ok() & (b % 2 == 0)
+        )
+        self.sends.start(
+            lambda: remote(north(), north(), xs.at[4, b], xs.at[5, b], dp=self.x_n), lambda: ok() & (b % 2 == 1)
+        )
+        self.sends.start(lambda: remote(east(), east(), cs.at[1, b], cs.at[5, b], dp=self.core_n), ok)
+        self.sends.start(lambda: remote(north(), north(), cs.at[2, b], cs.at[6, b], dp=self.core_n), ok)
+
+    def corner(self, b, ok):
+        far, xs, cs = (lambda: self.slot(self.diag, b)), self.xsem, self.csem
+        pl.when(ok())(lambda: remote(far(), far(), xs.at[4, b], xs.at[5, b], dp=self.x_n).wait_recv())
+        self.sends.start(lambda: remote(far(), far(), cs.at[3, b], cs.at[7, b], dp=self.core_n), ok)
+
+    def from_core(self):
+        shift = self.core_n - self.d
+        for b in range(self.parts):
+            for k, e in enumerate((self.d, self.x_n, self.y_n, self.diag)):
+                there = self.slot(e + shift, b)
+                remote(there, there, self.csem.at[k, b], self.csem.at[4 + k, b], dp=self.core_n).wait_recv()
+
+
+def enter_kernel(
+    spread, seq_ref, live_ref, tok_ref, w_ref, b_ref, up_ref, down_ref, ow_ref, ub_ref,
+    n1_ref, qx_ref, kx_ref, vx_ref, o_ref, heads_ref, full_ref,
+    wide, wq, piece, pack_ref, mask_ref, s_ref, nsem, hsem, own_sem, zsem, xsem, csem,
+):
+    rows, width = tok_ref.shape
+    unit = wide.shape[1]
+    blocks = parts = heads_ref.shape[0]
+    d, t = lax.axis_index("dp"), lax.axis_index("tensor")
+    barrier = greet(d, t, parts, spread)
+    sends = Sends()
     seq, live = seq_ref[0], live_ref[0]
     lane = lane_ids(rows)
     low = lane < HEAD
     row = lax.broadcasted_iota(jnp.int32, (rows, LANES), 0)
 
-    def project(i, carry):
-        at = pl.ds(pl.multiple_of(i * rows, rows), rows)
-        qkv = nn(n1_ref[at, :], w_ref[...]) + b_ref[...]
+    widen(tok_ref, wide)
+    x = wide[...]
+    s1, r = norm_stats(x, width + 1)
+    spare = lax.broadcasted_iota(jnp.int32, (rows, unit), 1) == width
+    n1_ref[at_rows(t, rows), :] = jnp.where(spare, 1.0, x * r).astype(BF)
+    barrier()
+
+    def line(b, up):
+        block = n1_ref.at[at_rows(b, rows), :]
+        return remote(block, block, nsem.at[1 if up else 2, b], nsem.at[0, b], tensor=t + 1 if up else t - 1)
+
+    def edge(up):
+        return t < parts - 1 if up else t > 0
+
+    def place(s, up):
+        b = t - s if up else t + s
+        return b, (lambda: t - s >= 0) if up else (lambda: t + s < parts)
+
+    places = {(s, up): place(s, up) for s in range(1, parts) for up in (True, False)}
+
+    for up in (True, False):
+        sends.start(lambda up=up: line(t, up), lambda up=up: edge(up))
+    for k in range(9):
+        take = 3 * (k % 2) + k // 2 if k < 6 else k
+        fill_rows(wq, w_ref[take * HEAD : (take + 1) * HEAD, :], k * HEAD, HEAD, width)
+    wq[9 * HEAD :, :] = jnp.zeros((HEAD, unit), BF)
+
+    if spread:
+        nd = 8
+        share, tail, qrow = unit // nd, 256 // nd, 640 // nd
+        near = share - 16
+        piece[:, unit - LANES :] = jnp.zeros((piece.shape[0], LANES), BF)
+        piece[:near, :] = up_ref[pl.ds(pl.multiple_of(d * share, 16), near), :]
+
+        @pl.when(d < nd - 1)
+        def _():
+            piece[near:share, :] = up_ref[pl.ds(pl.multiple_of(d * share + near, 16), 16), :]
+
+        @pl.when(d == nd - 1)
+        def _():
+            last = jnp.concatenate([up_ref[width - 15 :, :].astype(F32), ub_ref[...]], axis=0)
+            piece[near:share, :] = last.astype(BF)
+
+        piece[share : 2 * share, :width] = down_ref[pl.ds(pl.multiple_of(d * share, 16), share), :]
+
+        @pl.when(d < 6)
+        def _():
+            piece[2 * share : 2 * share + tail, :width] = ow_ref[pl.ds(pl.multiple_of(d * tail, 16), tail), :]
+
+        @pl.when(d >= 6)
+        def _():
+            piece[2 * share : 2 * share + tail, :] = jnp.zeros((tail, unit), BF)
+
+        piece[2 * share + tail :, :] = wq[pl.ds(pl.multiple_of(d * qrow, 16), qrow), :]
+        mine = pltpu.make_async_copy(piece, full_ref.at[d, t], own_sem.at[0])
+        mine.start()
+        gather = Spread(d, t, parts, piece, full_ref, zsem, xsem, csem, sends)
+        always = lambda: t >= 0
+        gather.plane(t, True, always)
+
+    def project(i):
+        at = at_rows(i, rows)
+        qkv = nt(n1_ref[at, :], wq[...]) + b_ref[...]
         qkv = qkv.astype(BF).astype(F32)
         key = row + i * rows
         m = lane - HEAD
@@ -111,9 +308,39 @@
             val = qkv[:, (3 + h // 2) * LANES : (4 + h // 2) * LANES]
             vx_ref[h, at, :] = jnp.where(low, half_turn(val) if h % 2 else val, ones).astype(BF)
         mask_ref[i] = diag_mask(i * rows, rows, live, False)
-        return carry
-
-    lax.fori_loop(0, blocks, project, 0)
+
+    for s in range(parts):
+        if s:
+            for up in (True, False):
+                b, ok = places[s, up]
+                pl.when(ok())(lambda b=b, up=up: line(b, up).wait_recv())
+                sends.start(lambda b=b, up=up: line(b, up), lambda ok=ok, up=up: ok() & edge(up))
+        if spread and s == 1:
+            gather.across(t, always)
+        if spread and s == 2:
+            gather.corner(t, always)
+
+        def arrived(e, carry, s=s):
+            b = t + (2 * e - 1) * s
+            pl.when((b >= 0) & (b < parts))(lambda: project(b))
+            return carry
+
+        lax.fori_loop(0, 2 if s else 1, arrived, 0)
+
+    if spread:
+        for up in (True, False):
+            gather.along(t, True, up, always)
+
+    def serve(k):
+        for up in (True, False):
+            if k + 1 < parts:
+                gather.from_z(*places[k + 1, up], up)
+        for up in (True, False):
+            if 1 <= k < parts:
+                gather.across(*places[k, up])
+        for up in (True, False):
+            if 2 <= k < parts + 1:
+                gather.corner(*places[k - 1, up])
 
     def head(h, carry):
         for i in range(blocks):
@@ -141,43 +368,82 @@
                 jnp.where(lane == HEAD + blocks + 1, mid, jnp.where(lane == HEAD + blocks + 2, lo, q.astype(F32))),
             )
             qx_ref[h, i * rows : (i + 1) * rows, :] = ext.astype(BF)
+        if spread:
+            for k in range(2):
+                pl.when(h == k)(partial(serve, k))
         return carry
 
     lax.fori_loop(0, 3, head, 0)
 
     def pack(i, carry):
-        at = pl.ds(pl.multiple_of(i * rows, rows), rows)
+        at = at_rows(i, rows)
         pack_ref[i, :rows, :] = jnp.where(low, o_ref[0, at, :], half_turn(o_ref[1, at, :])).astype(BF)
         pack_ref[i, rows:, :] = fold(o_ref[2, at, :]).astype(BF)
         return carry
 
     lax.fori_loop(0, blocks, pack, 0)
-
-
-def attend(seq, live, n1, w, b, blocks):
-    total = n1.shape[0]
-    rows = total // blocks
+    home = pltpu.make_async_copy(pack_ref.at[t], heads_ref.at[t], own_sem.at[1])
+    home.start()
+
+    def give(k):
+        to = lax.rem(t + k, parts)
+        return remote(pack_ref.at[to], heads_ref.at[t], hsem.at[0, k], hsem.at[1, k], tensor=to)
+
+    def take_in(k):
+        src = lax.rem(t + parts - k, parts)
+        return remote(pack_ref.at[src], heads_ref.at[src], hsem.at[0, k], hsem.at[1, k], tensor=src)
+
+    for k in (2, 1, 3):
+        sends.start(partial(give, k))
+    if spread:
+        for k in range(2, parts + 1):
+            serve(k)
+        gather.from_core()
+        mine.wait()
+    for k in range(1, parts):
+        take_in(k).wait_recv()
+    home.wait()
+    sends.finish()
+
+
+def enter(seq, live, tokens, w, b, up, down, ow, ub, parts, spread):
+    rows, width = tokens.shape
+    unit = width + 1
+    total = rows * parts
     ext = jax.ShapeDtypeStruct((3, total, LANES), BF)
+    pack = (parts, rows + rows // 2, LANES)
+    high = 2 * (unit // 8) + 256 // 8 + 640 // 8
+    dma = lambda *shape: pltpu.SemaphoreType.DMA(shape)
     return pl.pallas_call(
-        attend_kernel,
+        partial(enter_kernel, spread),
         out_shape=(
+            jax.ShapeDtypeStruct((total, unit), BF),
             ext,
             ext,
             ext,
             jax.ShapeDtypeStruct((3, total, LANES), F32),
-            jax.ShapeDtypeStruct((blocks, rows + rows // 2, LANES), BF),
+            jax.ShapeDtypeStruct(pack, BF),
+            jax.ShapeDtypeStruct((8, parts, high, unit) if spread else (8, 128), BF),
         ),
-        in_specs=[SMEM, SMEM, VMEM, VMEM, VMEM],
-        out_specs=(VMEM,) * 5,
-        scratch_shapes=[pltpu.VMEM((blocks, rows, rows), F32), pltpu.VMEM((blocks, rows, rows), F32)],
-        compiler_params=pltpu.CompilerParams(vmem_limit_bytes=LIMIT),
-    )(seq, live, n1, w, b)
+        in_specs=[SMEM, SMEM] + [VMEM] * 7,
+        out_specs=(VMEM,) * 6 + (ANY,),
+        scratch_shapes=[
+            pltpu.VMEM((rows, unit), F32),
+            pltpu.VMEM((640, unit), BF),
+            pltpu.VMEM((high, unit), BF),
+            pltpu.VMEM(pack, BF),
+            pltpu.VMEM((parts, rows, rows), F32),
+            pltpu.VMEM((parts, rows, rows), F32),
+            dma(3, parts), dma(2, parts), dma(2), dma(3, parts), dma(6, parts), dma(8, parts),
+        ],
+        compiler_params=pltpu.CompilerParams(vmem_limit_bytes=LIMIT, collective_id=0, has_side_effects=True),
+    )(seq, live, tokens, w, b, up, down, ow, ub)
 
 
 def middle_kernel(
     width, heads_ref, tok_ref, cot_ref, full_ref, ob_ref, db_ref,
     mixed_ref, hid_ref, hg_ref, grad_ref,
-    wu, wd, wm, wb, wo, wide, xall, n2_ref, gb_ref, dn_ref, sem,
+    wu, wd, wm, wo, wide, xall, n2_ref, gb_ref, dn_ref, sem,
 ):
     parts, rows = heads_ref.shape[0], tok_ref.shape[0]
     nd, piece = wu.shape[1:3]
@@ -185,13 +451,10 @@
     tail = grad_ref.shape[2] - 2 * piece
 
     def fetch(t, k):
-        if k == 3:
-            source = full_ref.at[0, t, pl.ds(3 * piece, 16), :]
-        else:
-            source = full_ref.at[:, t, pl.ds(k * piece, piece), :]
-        return pltpu.make_async_copy(source, (wu, wd, wm, wb)[k].at[t], sem.at[t, k])
-
-    for k in (2, 0, 1, 3):
+        source = full_ref.at[:, t, pl.ds(k * piece, tail if k == 2 else piece), :]
+        return pltpu.make_async_copy(source, (wu, wd, wm)[k].at[t], sem.at[t, k])
+
+    for k in (2, 0, 1):
         for t in range(parts):
             fetch(t, k).start()
     low = lane_ids(rows) < HEAD
@@ -204,13 +467,14 @@
         xall[:, (parts + k) * LANES : (parts + k + 1) * LANES] = both.astype(BF)
     for t in range(parts):
         fetch(t, 2).wait()
-        own = wm[t].reshape(unit, unit)
+        own = wm[t].reshape(tail * nd, unit)
         wo[t * LANES : (t + 1) * LANES, :] = own[:LANES]
         wo[parts * LANES + t * HEAD : parts * LANES + (t + 1) * HEAD, :] = own[LANES : LANES + HEAD]
     widen(tok_ref, wide)
     hidden = wide[...] + nn(xall[...], wo[...]) + ob_ref[...]
     s1, r = norm_stats(hidden, width + 1)
-    n2_ref[...] = (hidden * r).astype(BF)
+    spare = lax.broadcasted_iota(jnp.int32, (rows, unit), 1) == width
+    n2_ref[...] = jnp.where(spare, 1.0, hidden * r).astype(BF)
     hid_ref[...] = hidden
     widen(cot_ref, wide)
     gb_ref[...] = wide[...].astype(BF)
@@ -219,22 +483,19 @@
     root = (2 / jnp.pi) ** 0.5
 
     def unit_block(t, carry):
-        for k in (0, 1, 3):
+        for k in (0, 1):
             fetch(t, k).wait()
         up = wu[t].reshape(unit, unit)
         down = wd[t].reshape(unit, unit)
-        u = nn(n2_ref[...], up) + wb[t].astype(F32)[:1]
+        u = nn(n2_ref[...], up)
         th = jnp.tanh(root * (u + 0.044715 * (u * u * u)))
         act = (0.5 * u * (1 + th)).astype(BF)
         slope = 0.5 * (1 + th) + (0.5 * u) * (1 - th * th) * (root * (1 + 0.134145 * (u * u)))
         wide[...] += nn(act, down)
-        ug32 = nt(gb_ref[...], down) * slope
-        ug = ug32.astype(BF)
+        ug = (nt(gb_ref[...], down) * slope).astype(BF)
         dn_ref[...] += nt(ug, up)
-        bias_grad = jnp.sum(ug.astype(F32), axis=0, keepdims=True)
         grad_ref[:, t, :piece, :] = tn(n2_ref[...], ug).astype(BF).reshape(nd, piece, unit)
         grad_ref[:, t, piece : 2 * piece, :] = tn(act, gb_ref[...]).astype(BF).reshape(nd, piece, unit)
-        grad_ref[nd - 1, t, 2 * piece :, :] = jnp.broadcast_to(bias_grad, (tail, unit)).astype(BF)
         return carry
 
     lax.fori_loop(0, parts, unit_block, 0)
@@ -255,10 +516,7 @@
     last = tail * nd - (LANES + HEAD)
     spot = lax.broadcasted_iota(jnp.int32, (last, unit), 0)
     for t in range(parts):
-        ubg = grad_ref[nd - 1, t, 2 * piece :, :].astype(F32)[:1]
-        extra = jnp.where(
-            spot == 0, ubg, jnp.where(spot == 1, out_bias_grad, jnp.where(spot == 2, down_bias_grad, 0.0))
-        )
+        extra = jnp.where(spot == 0, out_bias_grad, jnp.where(spot == 1, down_bias_grad, 0.0))
         own = jnp.concatenate(
             [og[t * LANES : (t + 1) * LANES], og[parts * LANES + t * HEAD : parts * LANES + (t + 1) * HEAD], extra],
             axis=0,
@@ -286,11 +544,11 @@
         in_specs=[VMEM, VMEM, VMEM, ANY, VMEM, VMEM],
         out_specs=(VMEM,) * 4,
         scratch_shapes=[
-            weight, weight, weight,
-            pltpu.VMEM((parts, 16, unit), BF),
+            weight, weight,
+            pltpu.VMEM((parts, nd, tail, unit), BF),
             pltpu.VMEM((unit, unit), BF),
             square, half, half, half, square,
-            pltpu.SemaphoreType.DMA((parts, 4)),
+            pltpu.SemaphoreType.DMA((parts, 3)),
         ],
         compiler_params=pltpu.CompilerParams(vmem_limit_bytes=LIMIT),
     )(heads, tokens, cotangent, full, out_bias, down_bias)
@@ -361,13 +619,8 @@
         return carry
 
     lax.fori_loop(0, blocks, pack, 0)
-    spot = lax.broadcasted_iota(jnp.int32, (n1_ref.shape[1], LANES), 0)
     for k, m in enumerate((0, 1, 2, 3, 5)):
-        g = grads[m].astype(BF)
-        tall = jnp.sum(g.astype(F32), axis=0, keepdims=True)
-        wg_ref[:, k * LANES : (k + 1) * LANES] = jnp.where(
-            spot == n1_ref.shape[1] - 1, tall, tn(n1_ref[...], g)
-        )
+        wg_ref[k * LANES : (k + 1) * LANES, :] = tn(grads[m].astype(BF), n1_ref[...])
 
 
 def attend_back(live, n1, qx, kx, vx, o, hg):
@@ -378,7 +631,7 @@
         attend_back_kernel,
         out_shape=(
             jax.ShapeDtypeStruct((blocks, 4 * rows + rows // 2, LANES), BF),
-            jax.ShapeDtypeStruct((unit, 5 * LANES), F32),
+            jax.ShapeDtypeStruct((5 * LANES, unit), F32),
         ),
         in_specs=[SMEM] + [VMEM] * 6,
         out_specs=(VMEM, VMEM),
@@ -395,20 +648,23 @@
 
 def final_kernel(width, tok_ref, hid_ref, pack_ref, full_ref, out_ref, wm, wide, dn_ref, xt, sem):
     parts, rows = pack_ref.shape[0], tok_ref.shape[0]
-    nd, piece = wm.shape[1:3]
-    unit = piece * nd
+    nd, qrow, unit = wm.shape[1:]
+    first = full_ref.shape[2] - qrow
+
+    def fetch(t):
+        return pltpu.make_async_copy(full_ref.at[:, t, pl.ds(first, qrow), :], wm.at[t], sem.at[t])
+
     for t in range(parts):
-        pltpu.make_async_copy(full_ref.at[:, t, pl.ds(2 * piece, piece), :], wm.at[t], sem.at[t]).start()
+        fetch(t).start()
     widen(tok_ref, wide)
     dn_ref[...] = jnp.zeros_like(dn_ref)
 
     def part(t, carry):
-        pltpu.make_async_copy(full_ref.at[:, t, pl.ds(2 * piece, piece), :], wm.at[t], sem.at[t]).wait()
-        w = wm[t].reshape(unit, unit)[LANES + HEAD :]
+        fetch(t).wait()
         for k in range(4):
             xt[:, k * LANES : (k + 1) * LANES] = pack_ref[t, k * rows : (k + 1) * rows, :]
         xt[:, 4 * LANES :] = unfold(pack_ref[t, 4 * rows :, :].astype(F32)).astype(BF)
-        dn_ref[...] += nn(xt[:, : 9 * HEAD], w)
+        dn_ref[...] += nn(xt[...], wm[t].reshape(nd * qrow, unit))
         return carry
 
     lax.fori_loop(0, parts, part, 0)
@@ -428,7 +684,7 @@
         in_specs=[VMEM, VMEM, VMEM, ANY],
         out_specs=VMEM,
         scratch_shapes=[
-            pltpu.VMEM((parts, nd, unit // nd, unit), BF),
+            pltpu.VMEM((parts, nd, 640 // nd, unit), BF),
             pltpu.VMEM((rows, unit), F32),
             pltpu.VMEM((rows, unit), F32),
             pltpu.VMEM((rows, 5 * LANES), BF),
@@ -442,19 +698,10 @@
     return lax.all_to_all(x, "tensor", 0, 0, tiled=True)
 
 
-def pair_order(w):
-    w = w.reshape(w.shape[:-1] + (3, HEAD))
-    front = jnp.swapaxes(w[..., :2, :, :], -3, -2)
-    lead = w.shape[:-3]
-    return jnp.concatenate([front.reshape(lead + (6 * HEAD,)), w[..., 2, :, :].reshape(lead + (3 * HEAD,))], axis=-1)
-
-
-def pair_disorder(g):
-    lead = g.shape[:-1]
-    front = jnp.swapaxes(g[..., : 6 * HEAD].reshape(lead + (3, 2, HEAD)), -3, -2)
-    return jnp.concatenate([front, g[..., 6 * HEAD :].reshape(lead + (1, 3, HEAD))], axis=-3).reshape(
-        lead + (3, 3 * HEAD)
-    )
+def pair_rows(w, axis):
+    heads = [lax.slice_in_dim(w, k * HEAD, (k + 1) * HEAD, axis=axis) for k in range(9)]
+    order = [heads[3 * (k % 2) + k // 2] for k in range(6)] + heads[6:] + [jnp.zeros_like(heads[0])]
+    return jnp.concatenate(order, axis=axis)
 
 
 def local(
@@ -473,40 +720,25 @@
     down_bias,
 ):
     parts = groups["tensor"]
-    nd = 8 if groups["dp"] == 8 else 1
+    spread = groups["dp"] == 8
+    nd = 8 if spread else 1
     rows, width = tokens.shape
     unit = width + 1
     piece = unit // nd
-    tail = 256 // nd
-    me = lax.axis_index("dp") * piece if nd > 1 else 0
-
-    wide_in = jnp.pad(tokens.astype(F32), ((0, 0), (0, 1)))
-    s1, r = norm_stats(wide_in, unit)
-    n1 = lax.all_gather((wide_in * r).astype(BF), "tensor", axis=0, tiled=True)
-
-    qkv_flat = pair_order(qkv_weight)
-    def rows_of(w):
-        return lax.dynamic_slice_in_dim(w, me, piece, 0)
-
-    up_rows = rows_of(jnp.pad(up_weight, ((0, 1), (0, 0))))
-    down_rows = jnp.pad(rows_of(down_weight), ((0, 0), (0, 1)))
-    misc = jnp.pad(jnp.concatenate([out_weight, qkv_flat.T], axis=0), ((0, 0), (0, 1)))
-    bias_rows = jnp.broadcast_to(up_bias[None], (16, unit))
-    full = lax.all_gather(
-        jnp.concatenate([up_rows, down_rows, rows_of(misc), bias_rows], axis=0),
-        BOTH if nd > 1 else "tensor",
-        axis=0,
-        tiled=False,
-    ).reshape(nd, parts, 3 * piece + 16, unit)
-
-    w = jnp.pad(qkv_flat, ((0, 1), (0, HEAD)))
-    zero = jnp.zeros_like(qv_bias[0])
-    b = jnp.pad(pair_order(jnp.stack([qv_bias[0], zero, qv_bias[1]])), (0, HEAD)).astype(F32)[None]
-    qx, kx, vx, o, heads = attend(seq_length, live_rows, n1, w, b, parts)
-    heads = swap(heads)
-    as_row = lambda v: jnp.pad(v.astype(F32), (0, 1))[None]
-    mixed, hidgrad, hg, grads = middle(heads, tokens, cotangent, full, as_row(out_bias), as_row(down_bias))
-    if nd > 1:
+    as_row = lambda v: v.astype(F32)[None]
+
+    w = jnp.transpose(qkv_weight, (1, 2, 0)).reshape(9 * HEAD, width)
+    b = pair_rows(jnp.concatenate([qv_bias[0], jnp.zeros_like(qv_bias[0]), qv_bias[1]]).astype(F32), 0)[None]
+    n1, qx, kx, vx, o, heads, full = enter(
+        seq_length, live_rows, tokens, w, b, up_weight, down_weight, out_weight, as_row(up_bias), parts, spread
+    )
+    if not spread:
+        wide = lambda v, tall=0: jnp.pad(v, ((0, tall), (0, unit - v.shape[1])))
+        own = [jnp.concatenate([up_weight, up_bias[None]]), wide(down_weight), wide(out_weight, 64), wide(pair_rows(w, 0))]
+        full = lax.all_gather(jnp.concatenate(own), "tensor", axis=0, tiled=False)[None]
+    wide_row = lambda v: jnp.pad(as_row(v), ((0, 0), (0, 1)))
+    mixed, hidgrad, hg, grads = middle(heads, tokens, cotangent, full, wide_row(out_bias), wide_row(down_bias))
+    if spread:
         mine = lax.psum_scatter(grads, "dp", scatter_dimension=0, tiled=False)
         mine = lax.psum_scatter(mine, "tensor", scatter_dimension=0, tiled=False)
         mine = lax.all_gather(mine, "dp", axis=0, tiled=False)
@@ -516,22 +748,24 @@
     pack, wg = attend_back(live_rows, n1, qx, kx, vx, o, swap(hg))
     token_grad = final(tokens, hidgrad, swap(pack), full)
     wg = lax.psum(wg, "dp")
-    up_grad = mine[:, :piece].reshape(unit, unit)[:width].astype(F32)
+    up_grad = mine[:, :piece].reshape(unit, unit).astype(F32)
     down_grad = mine[:, piece : 2 * piece].reshape(unit, unit)[:, :width].astype(F32)
     rest = mine[:, 2 * piece :].reshape(256, unit).astype(F32)
-    out_grad = rest[: 3 * HEAD, :width]
-    wg = pair_disorder(wg[:, : 9 * HEAD])
+    wg = jnp.concatenate(
+        [wg[(2 * k if k < 3 else 2 * k - 5 if k < 6 else k) * HEAD :][:HEAD] for k in range(9)]
+    )
+    biases = wg[:, width].reshape(3, 3 * HEAD)
     return (
         mixed,
         token_grad,
-        wg[:width],
-        jnp.stack([wg[width, 0], wg[width, 2]]),
-        out_grad,
+        jnp.transpose(wg[:, :width].reshape(3, 3 * HEAD, width), (2, 0, 1)),
+        jnp.stack([biases[0], biases[2]]),
+        rest[: 3 * HEAD, :width],
+        rest[3 * HEAD, :width],
+        up_grad[:width],
+        up_grad[width],
+        down_grad,
         rest[3 * HEAD + 1, :width],
-        up_grad,
-        rest[3 * HEAD],
-        down_grad,
-        rest[3 * HEAD + 2, :width],
     )
 
 

time: 493 us -> 433 us (0.88)
  waiting for transfers between devices: 297 us -> 153 us
  Pallas kernels: 95.7 us -> 198 us
  local copies, waits for them, and re-layouts: 22.3 us -> 15.7 us
  other arithmetic: 9.83 us -> 3.34 us
    all_gather x2 -> x0, waiting for transfers between devices: 112 us -> none  [the longest x1 56.3 us: local(): n1 = lax.all_gather((wide_in * r).astype(BF), 'tensor', axis=0, tiled=True)]
    pallas_call x1, Pallas kernels: 23.7 us -> 130 us  [enter(): pl.pallas_call(partial(enter_kernel, spread), out_shape=(jax.ShapeDtypeSt...]
    all_to_all x2 -> x1, waiting for transfers between devices: 36.5 us -> 0.01 us  [swap(): return lax.all_to_all(x, 'tensor', 0, 0, tiled=True)]
    slice x14 -> x8, local copies, waits for them, and re-layouts: 9.89 us -> 5.21 us  [the longest x1 1.99 us: local(): wg[(2 * k if k < 3 else 2 * k - 5 if k < 6 else k) * HEAD:][:HEAD]]
  transfers between devices with their start and end apart: 8 -> 5, of which waited for: 6 -> 3; matrix products, arithmetic and copies ran while one was open for 3% -> 2% of each run, Pallas kernels for 13% -> 9%
where the time goes in v2:
time: 433 us
  Pallas kernels  198 us (46%)
  waiting for transfers between devices  153 us (35%)
  blocking collectives  43.4 us (10%)
  local copies, waits for them, and re-layouts  15.7 us (4%)
  between operations  15.2 us (4%)
    pallas_call x1, Pallas kernels, enter(): pl.pallas_call(partial(enter_kernel, spread), out_shape=(jax.ShapeDtypeSt...  130 us
    reduce_scatter x1, waiting for transfers between devices, local(): mine = lax.psum_scatter(grads, 'dp', scatter_dimension=0, tiled=False)  82.5 us
    psum x1, waiting for transfers between devices, local(): wg = lax.psum(wg, 'dp')  54.5 us
    all_to_all x1, blocking collectives, swap(): return lax.all_to_all(x, 'tensor', 0, 0, tiled=True)  43.4 us
    pallas_call x1, Pallas kernels, attend_back(): pl.pallas_call(attend_back_kernel, out_shape=(jax.ShapeDtypeStruct((block...  31.4 us
    pallas_call x1, Pallas kernels, middle(): pl.pallas_call(partial(middle_kernel, width), out_shape=(jax.ShapeDtypeSt...  28.3 us
    all_gather x1, waiting for transfers between devices, local(): mine = lax.all_gather(mine, 'dp', axis=0, tiled=False)  15.3 us
  transfers between devices with their start and end apart: 5, of which 3 were waited for; matrix products, arithmetic and copies ran while one was open for 2% of the time, Pallas kernels for 9%

profile of v2, /device:TPU:0, one launch (start us, length us, event | category | flops | bytes accessed | tf_op | source)
XLA Modules:
  0.0 432.7 jit_solution(9758015074806829215)
XLA Ops:
  7.2 0.8 slice_reduce_fusion.5
  9.6 0.6 broadcast_in_dim.24.b_ref
  10.2 0.7 broadcast_in_dim.27
  10.9 1.3 reshape.40.ub_ref
  12.2 0.7 broadcast_in_dim.28
  12.8 0.6 pad_convert_fusion
  13.4 130.1 %shard_map.195 = (bf16[2048,768]{1,0:T(8,128)(2,1)}, bf16[3,2048,128]{2,1,0:T(8,128)(2,1)}, bf16[3,2048,128]{2,1,0:T(8,128)(2,1)}, bf16[3,2048,128]{2,1,0:T(8,12...) custom-call(s32[1]{0:T(128)S(6)} %copy.28.seq_ref, ...), custom_call_target="tpu_custom_call" | custom-call | tf_op jit(solution)/shard_map/pallas_call | solution.py:417
  143.6 28.3 %shard_map.196 = (bf16[512,767]{1,0:T(8,128)(2,1)}, f32[512,768]{1,0:T(8,128)}, bf16[4,768,128]{2,1,0:T(8,128)(2,1)}, bf16[8,4,224,768]{3,2,1,0:T(8,128)(2,1)}) custom-call(bf16[4,768,128]{2,1,0:T(8,128)(2,1)} %get-tuple-element.23.heads_ref, bf16[512,767]{1,0:T(8,128)(2,1)} %tok_ref.5, bf16[512,767]{1,0:T(8,128)(2,1)} %cot_ref.1, ...), custom_call_target="tpu_custom_call" | custom-call | tf_op jit(solution)/shard_map/pallas_call | solution.py:536
  172.0 82.5 %reduce-scatter.3.cloned.1.call-done = bf16[1,4,224,768]{3,2,1,0:T(8,128)(2,1)} async-done(((bf16[8,4,224,768]{3,2,1,0:T(8,128)(2,1)}), bf16[1,4,224,768]{3,2,1,0:T(8,128)(2,1)}) %reduce-scatter.3.cloned.1.call-update) | async-done | bytes 1376272 | tf_op jit(solution)/shard_map/reduce_scatter | solution.py:742
  254.6 43.4 %all_to_all.10.hg_ref = bf16[4,768,128]{2,1,0:T(8,128)(2,1)} all-to-all(bf16[4,768,128]{2,1,0:T(8,128)(2,1)S(1)} %copy-done.4), channel_id=1, replica_groups=mesh['dp'=8,'tensor'=4] {'tensor'}, dimensions={0} | all-to-all | bytes 1572864 | tf_op jit(solution)/shard_map/all_to_all | solution.py:698
  298.0 31.4 %shard_map.197 = (bf16[4,2304,128]{2,1,0:T(8,128)(2,1)}, f32[640,768]{1,0:T(8,128)}) custom-call(s32[1]{0:T(128)S(6)} %copy.29.live_ref, bf16[2048,768]{1,0:T(8,128)(2,1)} %get-tuple-element.27.n1_ref, bf16[3,2048,128]{2,1,0:T(8,128)(2,1)} %get-tuple-element.28.qx_ref, bf16[3,2048,128]{2,1,0:T(8,128)(2,1)} %get-tuple-element.29.kx_ref, ...), custom_call_target="tpu_custom_call" | custom-call | tf_op jit(solution)/shard_map/pallas_call | solution.py:630
  329.5 0.5 all-gather.2.cloned.1.call-update
  330.0 3.8 all-to-all-start.1
  333.7 54.5 %all-reduce.4.cloned.1.call-done = f32[640,768]{1,0:T(8,128)} async-done(((f32[640,768]{1,0:T(8,128)}), f32[640,768]{1,0:T(8,128)}) %all-reduce.4.cloned.1.call-update) | async-done | bytes 1966096 | tf_op jit(solution)/shard_map/psum | solution.py:750
  388.2 2.0 fusion.2
  390.4 0.2 slice_reduce_fusion
  390.6 0.6 pad_maximum_fusion.2
  391.2 0.7 constant_dynamic-update-slice_fusion.1
  391.8 0.7 constant_dynamic-update-slice_fusion
  392.5 0.7 slice_dynamic-update-slice_fusion.2
  393.2 0.7 slice_dynamic-update-slice_fusion.1
  393.9 0.9 slice_dynamic-update-slice_fusion
  394.9 1.4 copy-done
  396.3 8.4 %shard_map.198 = bf16[512,767]{1,0:T(8,128)(2,1)} custom-call(bf16[512,767]{1,0:T(8,128)(2,1)} %tok_ref.5, f32[512,768]{1,0:T(8,128)} %get-tuple-element.26.hid_ref, bf16[4,2304,128]{2,1,0:T(8,128)(2,1)} %copy-done, bf16[8,4,304,768]{3,2,1,0:T(8,128)(2,1)} %get-tuple-element.24.full_ref), custom_call_target="tpu_custom_call" | custom-call | tf_op jit(solution)/shard_map/pallas_call | solution.py:681
  404.7 15.3 %all-gather.2.cloned.1.call-done = bf16[8,224,768]{2,1,0:T(8,128)(2,1)} async-done(((bf16[1,224,768]{2,1,0:T(8,128)(2,1)}), bf16[8,224,768]{2,1,0:T(8,128)(2,1)}) %all-gather.2.cloned.1.call-update) | async-done | bytes 2752528 | tf_op jit(solution)/shard_map/all_gather | solution.py:744
  420.0 1.2 slice.150
  421.2 0.6 slice_reduce_fusion.1
  421.9 0.9 slice.151
  422.9 1.6 slice_convert_fusion
  424.5 0.2 bitcast_convert_fusion
  424.7 0.7 slice_reduce_fusion.2
  425.4 0.7 copy-done.3
  (26 shorter events, 1.0 us)
Async XLA Ops:
  7.2 247.4 %reduce-scatter.3.cloned.1.call-start = ((), (), s32[]{:S(2)}) async-start(), calls=%async_computation.5 | async-start | bytes 12386304 | tf_op jit(solution)/shard_map/reduce_scatter | solution.py:742
  171.9 82.7 %copy-start.4 = (bf16[4,768,128]{2,1,0:T(8,128)(2,1)S(1)}, bf16[4,768,128]{2,1,0:T(8,128)(2,1)}, u32[]{:S(2)}) copy-start(bf16[4,768,128]{2,1,0:T(8,128)(2,1)} %get-tuple-element.32) | copy-start | bytes 2359300
  171.9 157.5 %reduce-scatter.5.cloned.1.call-start = ((), (), s32[]{:S(2)}) async-start(), calls=%async_computation.6 | async-start | bytes 1720320 | tf_op jit(solution)/shard_map/reduce_scatter | solution.py:743
  254.6 133.6 %all-reduce.4.cloned.1.call-start = ((), (), s32[]{:S(2)}) async-start(), calls=%async_computation.4 | async-start | bytes 3932160 | tf_op jit(solution)/shard_map/psum | solution.py:750
  329.4 90.6 %all-gather.2.cloned.1.call-start = ((), (), s32[]{:S(2)}) async-start(), calls=%async_computation.7 | async-start | bytes 3096576 | tf_op jit(solution)/shard_map/all_gather | solution.py:744
  330.0 64.9 %all-to-all-start.1 = ((bf16[4,2304,128]{2,1,0:T(8,128)(2,1)}), bf16[4,2304,128]{2,1,0:T(8,128)(2,1)S(1)}, u32[]{:S(2)}, u32[]{:S(2)}) async-start(bf16[4,2304,128]{2,1,0:T(8,128)(2,1)} %get-tuple-element.33), calls=%async_computation.1 | async-start | bytes 4718592 | tf_op jit(solution)/shard_map/all_to_all | solution.py:698
  388.2 2.2 copy-start.2
  394.9 1.4 copy-start
  420.0 2.7 copy-start.1
  424.7 1.4 copy-start.3
Sparse Core Ops, SparseCore 0:
  172.1 82.4 reduce-scatter.2
  256.8 44.2 reduce-scatter.4
  329.5 58.6 all-reduce.3
  390.1 29.8 all-gather.1
